TPU v7x, 128 devices: a whole 4x4x4 slice. The times are simulated.
128 devices in a mesh: ha: 8 (over z, x_lo), wa: 4 (over y), ta: 4 (over x_hi, core).
Axes of the slice: x: 4 (x_hi: 2, x_lo: 2; x = x_hi * 2 + x_lo), y: 4, z: 4, core: 2. Of those that a mesh axis runs over, the one named last changes fastest.
Arguments:
- queries: bfloat16 [12, 32, 64, 3072], P(None, 'wa', 'ha', 'ta'), may hold values from -10 to 10, as said below
- keys_values: bfloat16 [2, 12, 32, 64, 3072], P(None, None, 'wa', 'ha', 'ta'), may hold values from -6 to 6
- out_weight: bfloat16 [3072, 3072], P('ta'), may hold values from -2.5 to 2.5
Outputs:
- projected: bfloat16 [12, 32, 64, 3072], P(None, 'wa', 'ha', 'ta')
Inputs may be any that keep to these rules, and one draw needn't show every extreme that they name: `queries`: query entries.
All inputs are finite; a program needn't handle non-finite values.
Results may differ from a plain program's by a relative error of at most 0.013.
Values may be sent and summed in bfloat16 or wider, within the bound.
No kernel may reach another device: no remote copies, remote signals or barrier semaphores. Data moves between devices by JAX's collectives and lax.ppermute only.
A program may use at most 128 MiB of HBM per device.

v0:
```python
import functools

import jax
import jax.numpy as jnp
from jax import lax
from jax.experimental import pallas as pl
from jax.experimental.pallas import tpu as pltpu
from jax.sharding import PartitionSpec as P

HD = 128
LOG2E = 1.4426950408889634
EXP_SCALE = HD ** (-0.5) * LOG2E
LOW = -1e30
LIMIT = 2.0**60
KEYS = 256


COST2 = 1024
COST3 = 32


def attend_kernel(gates, first, last, step, *refs):
    flags_ref, q_ref = refs[:2]
    tiles = refs[2 : 2 + len(gates)]
    rest = refs[2 + len(gates) :]
    if not first:
        acc_in, top_in = rest[:2]
        rest = rest[2:]
    tokens = q_ref.shape[0]
    span = tiles[0].shape[1]
    inside = [None if gate is None else flags_ref[gate] > 0 for gate in gates]
    ones = jnp.ones((span, HD), jnp.bfloat16)

    def scores_of(queries, tile, begin, size):
        return lax.dot_general(
            queries, tile[0, pl.ds(begin, size), :], (((1,), (1,)), ((), ())),
            preferred_element_type=jnp.float32,
        )

    def row_max(scores):
        return jnp.broadcast_to(jnp.max(scores, axis=1, keepdims=True), (scores.shape[0], HD))

    def weights_of(scores, shift):
        wide = jnp.concatenate([shift] * (scores.shape[1] // HD), axis=1)
        return jnp.exp2((scores - wide) * EXP_SCALE).astype(jnp.bfloat16)

    def store(rows, mixed, top):
        if last:
            rest[0][rows, :] = (mixed[:, :HD] / mixed[:, HD:]).astype(rest[0].dtype)
        else:
            rest[0][rows, :] = mixed
            rest[1][rows, :] = top

    def full_step(start, all_scores):
        rows = pl.ds(start, step)
        old = jnp.full((step, HD), LOW, jnp.float32) if first else top_in[rows, :]
        new = old
        for scores, valid in zip(all_scores, inside):
            largest = row_max(scores)
            new = jnp.maximum(new, largest if valid is None else jnp.where(valid, largest, LOW))
        mixed = None
        for scores, valid, tile in zip(all_scores, inside, tiles):
            weights = weights_of(scores, new if valid is None else jnp.where(valid, new, -LOW))
            values = jnp.concatenate([tile[1], ones], axis=1)
            part = jnp.dot(weights, values, preferred_element_type=jnp.float32)
            mixed = part if mixed is None else mixed + part
        if not first:
            keep = jnp.exp2((old - new) * EXP_SCALE)
            mixed = acc_in[rows, :] * jnp.concatenate([keep, keep], axis=1) + mixed
        store(rows, mixed, new)

    def tile_scores(start):
        queries = q_ref[pl.ds(start, step), :]
        return [scores_of(queries, tile, 0, span) for tile in tiles]

    if first:
        ready = tile_scores(0)
        for start in range(0, tokens, step):
            following = tile_scores(start + step) if start + step < tokens else None
            full_step(start, ready)
            ready = following
        return

    def quick_weights(start):
        rows = pl.ds(start, step)
        queries = q_ref[rows, :]
        top = top_in[rows, :]
        parts = []
        for tile, valid in zip(tiles, inside):
            shift = top if valid is None else jnp.where(valid, top, -LOW)
            for begin in range(0, span, KEYS):
                parts.append(weights_of(scores_of(queries, tile, begin, KEYS), shift))
        return jnp.concatenate(parts, axis=1), top

    values = jnp.concatenate([jnp.concatenate([tile[1], ones], axis=1) for tile in tiles], axis=0)
    totals = None
    ready = quick_weights(0)
    for start in range(0, tokens, step):
        following = quick_weights(start + step) if start + step < tokens else None
        rows = pl.ds(start, step)
        mixed = jnp.dot(ready[0], values, preferred_element_type=jnp.float32)
        total = mixed[:, HD:]
        totals = total if totals is None else jnp.maximum(totals, total)
        store(rows, acc_in[rows, :] + mixed, ready[1])
        ready = following

    @pl.when(jnp.logical_not(jnp.max(totals) < LIMIT))
    def _():
        @pl.loop(0, tokens // step)
        def _(index):
            start = pl.multiple_of(index * step, step)
            full_step(start, tile_scores(start))


def attend(flags, queries, tiles, gates, state=None, last=False, part=None, cost=32):
    channels = queries.shape[1]
    tokens = queries.shape[0] if part is None else queries.shape[0] // 2
    heads = channels // HD
    span = queries.shape[0]
    arrays = [tile[0] if isinstance(tile, tuple) else tile for tile in tiles]

    def tile_spec(tile):
        if isinstance(tile, tuple):
            return pl.BlockSpec((None, 2, span, HD), lambda h: (tile[1], 0, 0, h))
        return pl.BlockSpec((2, span, HD), lambda h: (0, 0, h))

    def rows_spec(array, width):
        block = 0 if part is None or array.shape[0] == tokens else part
        return pl.BlockSpec((tokens, width), lambda h: (block, h))

    in_specs = [pl.BlockSpec(memory_space=pltpu.SMEM), rows_spec(queries, HD)] + [tile_spec(tile) for tile in tiles]
    args = [flags, queries, *arrays]
    if state is not None:
        in_specs += [rows_spec(state[0], 2 * HD), rows_spec(state[1], HD)]
        args += list(state)
    if last:
        out_shape = jax.ShapeDtypeStruct((tokens, channels), jnp.bfloat16)
        out_specs = rows_spec(out_shape, HD)
    else:
        out_shape = [
            jax.ShapeDtypeStruct((tokens, 2 * channels), jnp.float32),
            jax.ShapeDtypeStruct((tokens, channels), jnp.float32),
        ]
        out_specs = [rows_spec(out_shape[0], 2 * HD), rows_spec(out_shape[1], HD)]
    step = 256 if tokens % 256 == 0 else 192
    pairs = len(tiles) * heads * tokens * span
    return pl.pallas_call(
        functools.partial(attend_kernel, tuple(gates), state is None, last, step),
        out_shape=out_shape,
        grid=(heads,),
        in_specs=in_specs,
        out_specs=out_specs,
        compiler_params=pltpu.CompilerParams(vmem_limit_bytes=28 * 1024 * 1024),
        cost_estimate=pl.CostEstimate(flops=pairs * cost, bytes_accessed=1024, transcendentals=0),
    )(*args)


def body(queries, keys_values, out_weight):
    frames, rows, cols, channels = queries.shape
    tokens = frames * rows * cols
    half = channels // 2
    ha_count, wa_count = lax.axis_size("ha"), lax.axis_size("wa")
    ha, wa, ta = lax.axis_index("ha"), lax.axis_index("wa"), lax.axis_index("ta")
    odd = lax.rem(ha, 2)

    q_all = queries.reshape(tokens, channels)
    kv_all = keys_values.reshape(2, tokens, channels)
    keep_at, send_at = odd * half, (1 - odd) * half

    swap_pairs = [(i, i ^ 1) for i in range(ha_count)]
    native_pairs = [(i, (i + (2 if i % 2 else -2)) % ha_count) for i in range(ha_count)]
    swapped_pairs = [(i, (i + (-2 if i % 2 else 2)) % ha_count) for i in range(ha_count)]
    down_pairs = [(i, (i + 1) % wa_count) for i in range(wa_count)]
    up_pairs = [((i + 1) % wa_count, i) for i in range(wa_count)]

    def above_below(cells):
        return lax.ppermute(cells, "wa", down_pairs), lax.ppermute(cells, "wa", up_pairs)

    above, below = wa > 0, wa < wa_count - 1
    low, high = ha >= 2, ha < ha_count - 2
    far_partner = jnp.where(odd == 1, low, high)
    far_native = jnp.where(odd == 1, high, low)
    flags = jnp.stack(
        [above, below, far_partner, far_partner & above, far_partner & below,
         far_native, far_native & above, far_native & below]
    ).astype(jnp.int32)

    kv_send = lax.dynamic_slice_in_dim(kv_all, send_at, half, 2)
    kv_send, kv_all = lax.optimization_barrier((kv_send, kv_all))
    kv_own = lax.dynamic_slice_in_dim(kv_all, keep_at, half, 2)
    q_send = lax.dynamic_slice_in_dim(q_all, send_at, half, 1)
    q_own = lax.dynamic_slice_in_dim(q_all, keep_at, half, 1)

    core, x_hi = lax.rem(ta, 2), ta // 2
    width = out_weight.shape[1] // lax.axis_size("ta")
    ordered = jnp.concatenate(
        [lax.dynamic_slice_in_dim(out_weight, at, half, 0) for at in (keep_at, send_at)], axis=0
    )
    groups = (2 * (1 - x_hi) + 1 - core, 2 * (1 - x_hi) + core, 2 * x_hi + 1 - core, ta)
    weights = [lax.dynamic_slice_in_dim(ordered, group * width, width, 1) for group in groups]

    kv_pair = lax.ppermute(kv_send, "ha", swap_pairs)
    own_up, own_down = above_below(kv_own)
    far_p = lax.ppermute(kv_own, "ha", native_pairs)
    flags, *weights = lax.optimization_barrier((flags, *weights))
    state_n = attend(flags, q_own, [kv_own], [None])
    own_up, own_down, state_n = lax.optimization_barrier((own_up, own_down, state_n))
    far_p_rows = lax.ppermute(jnp.stack([own_up, own_down]), "ha", native_pairs)
    kv_pair, q_send, state_n, far_p = lax.optimization_barrier((kv_pair, q_send, state_n, far_p))
    q_pair = lax.ppermute(q_send, "ha", swap_pairs)
    pair_up, pair_down = above_below(kv_pair)
    far_n = lax.ppermute(kv_pair, "ha", swapped_pairs)

    state_n = attend(flags, q_own, [kv_pair, own_up, own_down], [None, 0, 1], state_n)
    q_pair, state_n = lax.optimization_barrier((q_pair, state_n))
    state_p = attend(flags, q_pair, [kv_own, kv_pair, own_up, own_down, far_p], [None, None, 0, 1, 2], cost=COST3)
    far_n, state_p = lax.optimization_barrier((far_n, state_p))
    far_n_up, far_n_down = above_below(far_n)
    state_p = attend(flags, q_pair, [pair_up, pair_down], [0, 1], state_p)
    state_n, state_p = lax.optimization_barrier((state_n, state_p))
    state_n = attend(flags, q_own, [pair_up, pair_down, far_n], [0, 1, 5], state_n)
    state_p, state_n = lax.optimization_barrier((state_p, state_n))
    backs = []
    for part in (0, 1):
        out_p = attend(
            flags, q_pair, [(far_p_rows, 0), (far_p_rows, 1)], [3, 4], state_p, last=True, part=part
        )
        state_p, state_n, out_p = lax.optimization_barrier((state_p, state_n, out_p))
        backs.append(lax.ppermute(out_p, "ha", swap_pairs))
    out_n = attend(flags, q_own, [far_n_up, far_n_down], [6, 7], state_n, last=True)
    back_0, back_1, out_n = lax.optimization_barrier((*backs, out_n))

    core_pairs = [(i, i ^ 1) for i in range(4)]
    hi_pairs = [(i, i ^ 2) for i in range(4)]

    attention = jnp.concatenate([out_n, jnp.concatenate([back_0, back_1], axis=0)], axis=1)

    def partial_of(group, start, stop):
        return jnp.dot(attention[start:stop], weights[group], preferred_element_type=jnp.float32)

    fars = []
    for start in (0, tokens // 2):
        stop = start + tokens // 2
        taken = lax.ppermute(partial_of(0, start, stop).astype(jnp.bfloat16), "ta", core_pairs)
        away = (partial_of(1, start, stop) + taken.astype(jnp.float32)).astype(jnp.bfloat16)
        fars.append(lax.ppermute(away, "ta", hi_pairs))
    home_taken = lax.ppermute(partial_of(2, 0, tokens).astype(jnp.bfloat16), "ta", core_pairs)
    home = partial_of(3, 0, tokens) + home_taken.astype(jnp.float32)
    result = home + jnp.concatenate(fars, axis=0).astype(jnp.float32)
    return result.astype(jnp.bfloat16).reshape(frames, rows, cols, width)


def solution(mesh):
    return jax.shard_map(
        body,
        mesh=mesh,
        in_specs=(P(None, "wa", "ha", "ta"), P(None, None, "wa", "ha", "ta"), P("ta", None)),
        out_specs=P(None, "wa", "ha", "ta"),
        check_vma=False,
    )
```

profile of v0, /device:TPU:1, one launch (start us, length us, event | category | flops | bytes accessed | tf_op | source)
XLA Modules:
  0.0 142.5 jit_solution(17661287359066515885)
XLA Ops:
  0.0 1.7 %copy-done = bf16[2,12,8,8,768]{4,3,2,1,0:T(8,128)(2,1)S(1)} copy-done((bf16[2,12,8,8,768]{4,3,2,1,0:T(8,128)(2,1)S(1)}, bf16[2,12,8,8,768]{4,3,2,1,0:T(8,128)(2,1)}, u32[]{:S(2)}) %copy-start) | copy-done | bytes 2359320
  1.7 1.1 constant_dynamic-slice_fusion.5
  2.9 2.2 %collective-permute-start.1 = (bf16[2,768,384]{2,1,0:T(8,128)(2,1)S(1)}, bf16[2,768,384]{2,1,0:T(8,128)(2,1)}, u32[]{:S(2)}, u32[]{:S(2)}) collective-permute-start(bf16[2,768,384]{2,1,0:T(8,128)(2,1)S(1)} %constant_dynamic-slice_fusion.3.refs_2_), channel_id=1, source_target_pairs={{0,4},{4,8},{8,12},{12,0},{1,5},{5,9},{9,13},{13,1},{2,6},{6,10},{... | collective-permute-start | bytes 3538952 | tf_op jit(solution)/shard_map/ppermute | solution.py:177
  5.1 1.5 %collective-permute-start.2 = (bf16[2,768,384]{2,1,0:T(8,128)(2,1)S(1)}, bf16[2,768,384]{2,1,0:T(8,128)(2,1)}, u32[]{:S(2)}, u32[]{:S(2)}) collective-permute-start(bf16[2,768,384]{2,1,0:T(8,128)(2,1)S(1)} %constant_dynamic-slice_fusion.3.refs_2_), channel_id=1, source_target_pairs={{4,0},{8,4},{12,8},{0,12},{5,1},{9,5},{13,9},{1,13},{6,2},{10,6},{... | collective-permute-start | bytes 3538952 | tf_op jit(solution)/shard_map/ppermute | solution.py:177
  6.6 3.8 %collective-permute-start.3 = (bf16[2,768,384]{2,1,0:T(8,128)(2,1)S(1)}, bf16[2,768,384]{2,1,0:T(8,128)(2,1)}, u32[]{:S(2)}, u32[]{:S(2)}) collective-permute-start(bf16[2,768,384]{2,1,0:T(8,128)(2,1)S(1)} %constant_dynamic-slice_fusion.3.refs_2_), channel_id=1, source_target_pairs={{0,96},{16,48},{32,0},{48,80},{64,32},{80,112},{96,64},{112,16},{1... | collective-permute-start | bytes 3538952 | tf_op jit(solution)/shard_map/ppermute | solution.py:204
  10.5 2.7 %constant_dynamic-slice_fusion.1 = (bf16[384,3072]{1,0:T(8,128)(2,1)S(1)}, bf16[384,3072]{1,0:T(8,128)(2,1)S(1)}) fusion(bf16[768,3072]{1,0:T(8,128)(2,1)} %param.5, s32[]{:T(128)S(6)} %select_n.34, s32[]{:T(128)S(6)} %select_n.35), kind=kLoop, calls=%fused_computation.27 | loop fusion | bytes 9437192 | tf_op jit(solution)/shard_map/dynamic_slice | solution.py:197
  14.6 4.1 %shard_map.37 = (f32[768,768]{1,0:T(8,128)S(1)}, f32[768,384]{1,0:T(8,128)S(1)}) custom-call(s32[8]{0:T(128)S(1)} %convert_element_type.33.refs_0_, bf16[768,384]{1,0:T(8,128)(2,1)S(1)} %get-tuple-element.113.refs_1_, bf16[2,768,384]{2,1,0:T(8,128)(2,1)S(1)} %constant_dynamic-slice_fusion.3.refs_2_), custom_call_target="tpu_custom_call" | custom-call | flops 56623104 | bytes 1024 | tf_op jit(solution)/shard_map/pallas_call | solution.py:147
  18.8 13.4 %collective-permute-done.1.refs_3_.refs_4_ = bf16[2,768,384]{2,1,0:T(8,128)(2,1)} collective-permute-done((bf16[2,768,384]{2,1,0:T(8,128)(2,1)S(1)}, bf16[2,768,384]{2,1,0:T(8,128)(2,1)}, u32[]{:S(2)}, u32[]{:S(2)}) %collective-permute-start.1) | collective-permute-done | bytes 1179680 | tf_op jit(solution)/shard_map/ppermute | solution.py:177
  32.2 1.9 %pad_maximum_fusion = bf16[2,2,768,384]{3,2,1,0:T(8,128)(2,1)S(1)} fusion(bf16[1,2,768,384]{3,2,1,0:T(8,128)(2,1)} %bitcast.11, bf16[1,2,768,384]{3,2,1,0:T(8,128)(2,1)} %bitcast.10), kind=kLoop, calls=%fused_computation.8 | loop fusion | flops 1179648 | bytes 4718592 | tf_op jit(solution)/shard_map/stack | solution.py:208
  34.1 3.7 %collective-permute-start.8 = (bf16[2,2,768,384]{3,2,1,0:T(8,128)(2,1)S(1)}, bf16[2,2,768,384]{3,2,1,0:T(8,128)(2,1)S(1)}, u32[]{:S(2)}, u32[]{:S(2)}) collective-permute-start(bf16[2,2,768,384]{3,2,1,0:T(8,128)(2,1)S(1)} %pad_maximum_fusion), channel_id=1, source_target_pairs={{0,96},{16,48},{32,0},{48,80},{64,32},{80,112},{96,64},{112,16},{1... | collective-permute-start | bytes 7077896 | tf_op jit(solution)/shard_map/ppermute | solution.py:208
  37.8 1.3 collective-permute-start.4
  39.1 0.9 collective-permute-start.5
  40.1 1.8 %collective-permute-start.6 = (bf16[2,768,384]{2,1,0:T(8,128)(2,1)}, bf16[2,768,384]{2,1,0:T(8,128)(2,1)S(1)}, u32[]{:S(2)}, u32[]{:S(2)}) collective-permute-start(bf16[2,768,384]{2,1,0:T(8,128)(2,1)} %collective-permute-done.refs_2_.refs_3_), channel_id=1, source_target_pairs={{4,0},{8,4},{12,8},{0,12},{5,1},{9,5},{13,9},{1,13},{6,2},{10,6},{... | collective-permute-start | bytes 3538952 | tf_op jit(solution)/shard_map/ppermute | solution.py:177
  41.8 8.1 %shard_map.38 = (f32[768,768]{1,0:T(8,128)S(1)}, f32[768,384]{1,0:T(8,128)S(1)}) custom-call(s32[8]{0:T(128)S(1)} %convert_element_type.33.refs_0_, bf16[768,384]{1,0:T(8,128)(2,1)S(1)} %get-tuple-element.113.refs_1_, bf16[2,768,384]{2,1,0:T(8,128)(2,1)} %collective-permute-done.refs_2_.refs_3_, bf16[2,768,384]{2,1,0:T(8,128)(2,1)} %collective-permute-done.1.refs_3_.refs_4_, ...), custom_call_target="tpu_custom_call" | custom-call | flops 169869312 | bytes 1024 | tf_op jit(solution)/shard_map/pallas_call | solution.py:147
  50.0 1.0 collective-permute-done.4.refs_1_
  51.0 12.7 %shard_map.39 = (f32[768,768]{1,0:T(8,128)S(1)}, f32[768,384]{1,0:T(8,128)S(1)}) custom-call(s32[8]{0:T(128)S(1)} %convert_element_type.33.refs_0_, bf16[768,384]{1,0:T(8,128)(2,1)S(1)} %collective-permute-done.4.refs_1_, bf16[2,768,384]{2,1,0:T(8,128)(2,1)S(1)} %constant_dynamic-slice_fusion.3.refs_2_, ...), custom_call_target="tpu_custom_call" | custom-call | flops 283115520 | bytes 1024 | tf_op jit(solution)/shard_map/pallas_call | solution.py:147
  63.7 1.2 collective-permute-done.7.refs_4_
  65.5 2.1 %collective-permute-start.12 = (bf16[2,768,384]{2,1,0:T(8,128)(2,1)S(1)}, bf16[2,768,384]{2,1,0:T(8,128)(2,1)S(1)}, u32[]{:S(2)}, u32[]{:S(2)}) collective-permute-start(bf16[2,768,384]{2,1,0:T(8,128)(2,1)S(1)} %collective-permute-done.7.refs_4_), channel_id=1, source_target_pairs={{4,0},{8,4},{12,8},{0,12},{5,1},{9,5},{13,9},{1,13},{6,2},{10,6},{... | collective-permute-start | bytes 3538952 | tf_op jit(solution)/shard_map/ppermute | solution.py:177
  67.6 6.0 %shard_map.40 = (f32[768,768]{1,0:T(8,128)S(1)}, f32[768,384]{1,0:T(8,128)S(1)}) custom-call(s32[8]{0:T(128)S(1)} %convert_element_type.33.refs_0_, bf16[768,384]{1,0:T(8,128)(2,1)S(1)} %collective-permute-done.4.refs_1_, bf16[2,768,384]{2,1,0:T(8,128)(2,1)S(1)} %collective-permute-done.5.refs_2_, bf16[2,768,384]{2,1,0:T(8,128)(2,1)S(1)} %collective-permute-done.6.refs_3_, ...), custom_call_target="tpu_custom_call" | custom-call | flops 113246208 | bytes 1024 | tf_op jit(solution)/shard_map/pallas_call | solution.py:147
  73.6 7.9 %shard_map.41 = (f32[768,768]{1,0:T(8,128)S(1)}, f32[768,384]{1,0:T(8,128)S(1)}) custom-call(s32[8]{0:T(128)S(1)} %convert_element_type.33.refs_0_, bf16[768,384]{1,0:T(8,128)(2,1)S(1)} %get-tuple-element.113.refs_1_, bf16[2,768,384]{2,1,0:T(8,128)(2,1)S(1)} %collective-permute-done.5.refs_2_, bf16[2,768,384]{2,1,0:T(8,128)(2,1)S(1)} %collective-permute-done.6.refs_3_, ...), custom_call_target="tpu_custom_call" | custom-call | flops 169869312 | bytes 1024 | tf_op jit(solution)/shard_map/pallas_call | solution.py:147
  81.5 5.3 %collective-permute-done.8.refs_2_.refs_3_ = bf16[2,2,768,384]{3,2,1,0:T(8,128)(2,1)S(1)} collective-permute-done((bf16[2,2,768,384]{3,2,1,0:T(8,128)(2,1)S(1)}, bf16[2,2,768,384]{3,2,1,0:T(8,128)(2,1)S(1)}, u32[]{:S(2)}, u32[]{:S(2)}) %collective-permute-start.8) | collective-permute-done | bytes 2359328 | tf_op jit(solution)/shard_map/ppermute | solution.py:208
  86.9 3.8 %shard_map.42 = bf16[384,384]{1,0:T(8,128)(2,1)S(1)} custom-call(s32[8]{0:T(128)S(1)} %convert_element_type.33.refs_0_, bf16[768,384]{1,0:T(8,128)(2,1)S(1)} %collective-permute-done.4.refs_1_, bf16[2,2,768,384]{3,2,1,0:T(8,128)(2,1)S(1)} %collective-permute-done.8.refs_2_.refs_3_, bf16[2,2,768,384]{3,2,1,0:T(8,128)(2,1)S(1)} %collective-permute-done.8.refs_2_.refs_3_, ...), custom_call_target="tpu_custom_call" | custom-call | flops 56623104 | bytes 1024 | tf_op jit(solution)/shard_map/pallas_call | solution.py:147
  90.7 2.3 %collective-permute-start.9 = (bf16[384,384]{1,0:T(8,128)(2,1)S(1)}, bf16[384,384]{1,0:T(8,128)(2,1)S(1)}, u32[]{:S(2)}, u32[]{:S(2)}) collective-permute-start(bf16[384,384]{1,0:T(8,128)(2,1)S(1)} %shard_map.42), channel_id=1, source_target_pairs={{0,16},{16,0},{32,48},{48,32},{64,80},{80,64},{96,112},{112,96},{1... | collective-permute-start | bytes 884744 | tf_op jit(solution)/shard_map/ppermute | solution.py:229
  93.0 3.8 %shard_map.43 = bf16[384,384]{1,0:T(8,128)(2,1)S(1)} custom-call(s32[8]{0:T(128)S(1)} %convert_element_type.33.refs_0_, bf16[768,384]{1,0:T(8,128)(2,1)S(1)} %collective-permute-done.4.refs_1_, bf16[2,2,768,384]{3,2,1,0:T(8,128)(2,1)S(1)} %collective-permute-done.8.refs_2_.refs_3_, bf16[2,2,768,384]{3,2,1,0:T(8,128)(2,1)S(1)} %collective-permute-done.8.refs_2_.refs_3_, ...), custom_call_target="tpu_custom_call" | custom-call | flops 56623104 | bytes 1024 | tf_op jit(solution)/shard_map/pallas_call | solution.py:147
  97.2 5.8 %shard_map.44 = bf16[768,384]{1,0:T(8,128)(2,1)S(1)} custom-call(s32[8]{0:T(128)S(1)} %convert_element_type.33.refs_0_, bf16[768,384]{1,0:T(8,128)(2,1)S(1)} %get-tuple-element.113.refs_1_, bf16[2,768,384]{2,1,0:T(8,128)(2,1)S(1)} %collective-permute-done.11.refs_2_, bf16[2,768,384]{2,1,0:T(8,128)(2,1)S(1)} %collective-permute-done.12.refs_3_, ...), custom_call_target="tpu_custom_call" | custom-call | flops 113246208 | bytes 1024 | tf_op jit(solution)/shard_map/pallas_call | solution.py:147
  103.0 1.6 %collective-permute-done.10 = bf16[384,384]{1,0:T(8,128)(2,1)S(1)} collective-permute-done((bf16[384,384]{1,0:T(8,128)(2,1)S(1)}, bf16[384,384]{1,0:T(8,128)(2,1)S(1)}, u32[]{:S(2)}, u32[]{:S(2)}) %collective-permute-start.10) | collective-permute-done | bytes 294944 | tf_op jit(solution)/shard_map/ppermute | solution.py:229
  105.4 2.7 %collective-permute-start.16 = (bf16[384,768]{1,0:T(8,128)(2,1)S(1)}, bf16[384,768]{1,0:T(8,128)(2,1)S(1)}, u32[]{:S(2)}, u32[]{:S(2)}) collective-permute-start(bf16[384,768]{1,0:T(8,128)(2,1)S(1)} %convolution_convert_fusion.1), channel_id=1, source_target_pairs={{0,1},{1,0},{2,3},{3,2},{4,5},{5,4},{6,7},{7,6},{8,9},{9,8},{10,11... | collective-permute-start | bytes 1769480 | tf_op jit(solution)/shard_map/ppermute | solution.py:244
  108.8 1.1 convolution_convert_fusion
  111.1 2.5 %collective-permute-start.17 = (bf16[384,768]{1,0:T(8,128)(2,1)S(1)}, bf16[384,768]{1,0:T(8,128)(2,1)S(1)}, u32[]{:S(2)}, u32[]{:S(2)}) collective-permute-start(bf16[384,768]{1,0:T(8,128)(2,1)S(1)} %add_convert_fusion.1), channel_id=1, source_target_pairs={{0,2},{1,3},{2,0},{3,1},{4,6},{5,7},{6,4},{7,5},{8,10},{9,11},{10,... | collective-permute-start | bytes 1769480 | tf_op jit(solution)/shard_map/ppermute | solution.py:246
  114.9 12.8 %collective-permute-done.17 = bf16[384,768]{1,0:T(8,128)(2,1)S(1)} collective-permute-done((bf16[384,768]{1,0:T(8,128)(2,1)S(1)}, bf16[384,768]{1,0:T(8,128)(2,1)S(1)}, u32[]{:S(2)}, u32[]{:S(2)}) %collective-permute-start.17) | collective-permute-done | bytes 589856 | tf_op jit(solution)/shard_map/ppermute | solution.py:246
  127.7 12.6 %collective-permute-done.15 = bf16[384,768]{1,0:T(8,128)(2,1)S(1)} collective-permute-done((bf16[384,768]{1,0:T(8,128)(2,1)S(1)}, bf16[384,768]{1,0:T(8,128)(2,1)S(1)}, u32[]{:S(2)}, u32[]{:S(2)}) %collective-permute-start.15) | collective-permute-done | bytes 589856 | tf_op jit(solution)/shard_map/ppermute | solution.py:246
  140.3 2.2 %add_convert_fusion = bf16[768,768]{1,0:T(8,128)(2,1)} fusion(bf16[768,768]{1,0:T(8,128)(2,1)S(1)} %collective-permute-done.13, bf16[384,768]{1,0:T(8,128)(2,1)S(1)} %collective-permute-done.17, bf16[384,768]{1,0:T(8,128)(2,1)S(1)} %collective-permute-done.15, bf16[768,768]{1,0:T(8,128)(2,1)S(1)} %get-tuple-element.103, ...), kind=kOutput, calls=%fused_computation.9 | convolution fusion | flops 914227200 | bytes 5898240 | tf_op jit(solution)/shard_map/dot_general | solution.py:239
  (31 shorter events, 6.5 us)
Async XLA Ops:
  0.0 1.7 %copy-start = (bf16[2,12,8,8,768]{4,3,2,1,0:T(8,128)(2,1)S(1)}, bf16[2,12,8,8,768]{4,3,2,1,0:T(8,128)(2,1)}, u32[]{:S(2)}) copy-start(bf16[2,12,8,8,768]{4,3,2,1,0:T(8,128)(2,1)} %param.4) | copy-start | bytes 7077892
  2.9 29.3 %collective-permute-start.1 = (bf16[2,768,384]{2,1,0:T(8,128)(2,1)S(1)}, bf16[2,768,384]{2,1,0:T(8,128)(2,1)}, u32[]{:S(2)}, u32[]{:S(2)}) collective-permute-start(bf16[2,768,384]{2,1,0:T(8,128)(2,1)S(1)} %constant_dynamic-slice_fusion.3.refs_2_), channel_id=1, source_target_pairs={{0,4},{4,8},{8,12},{12,0},{1,5},{5,9},{9,13},{13,1},{2,6},{6,10},{... | collective-permute-start | bytes 3538952 | tf_op jit(solution)/shard_map/ppermute | solution.py:177
  5.1 27.1 %collective-permute-start.2 = (bf16[2,768,384]{2,1,0:T(8,128)(2,1)S(1)}, bf16[2,768,384]{2,1,0:T(8,128)(2,1)}, u32[]{:S(2)}, u32[]{:S(2)}) collective-permute-start(bf16[2,768,384]{2,1,0:T(8,128)(2,1)S(1)} %constant_dynamic-slice_fusion.3.refs_2_), channel_id=1, source_target_pairs={{4,0},{8,4},{12,8},{0,12},{5,1},{9,5},{13,9},{1,13},{6,2},{10,6},{... | collective-permute-start | bytes 3538952 | tf_op jit(solution)/shard_map/ppermute | solution.py:177
  6.6 31.2 %collective-permute-start.3 = (bf16[2,768,384]{2,1,0:T(8,128)(2,1)S(1)}, bf16[2,768,384]{2,1,0:T(8,128)(2,1)}, u32[]{:S(2)}, u32[]{:S(2)}) collective-permute-start(bf16[2,768,384]{2,1,0:T(8,128)(2,1)S(1)} %constant_dynamic-slice_fusion.3.refs_2_), channel_id=1, source_target_pairs={{0,96},{16,48},{32,0},{48,80},{64,32},{80,112},{96,64},{112,16},{1... | collective-permute-start | bytes 3538952 | tf_op jit(solution)/shard_map/ppermute | solution.py:204
  10.4 27.4 %collective-permute-start = (bf16[2,768,384]{2,1,0:T(8,128)(2,1)}, bf16[2,768,384]{2,1,0:T(8,128)(2,1)}, u32[]{:S(2)}, u32[]{:S(2)}) collective-permute-start(bf16[2,768,384]{2,1,0:T(8,128)(2,1)} %constant_dynamic-slice_fusion.5), channel_id=1, source_target_pairs={{0,16},{16,0},{32,48},{48,32},{64,80},{80,64},{96,112},{112,96},{1... | collective-permute-start | bytes 3538952 | tf_op jit(solution)/shard_map/ppermute | solution.py:202
  13.2 1.3 copy-start.1
  34.1 52.8 %collective-permute-start.8 = (bf16[2,2,768,384]{3,2,1,0:T(8,128)(2,1)S(1)}, bf16[2,2,768,384]{3,2,1,0:T(8,128)(2,1)S(1)}, u32[]{:S(2)}, u32[]{:S(2)}) collective-permute-start(bf16[2,2,768,384]{3,2,1,0:T(8,128)(2,1)S(1)} %pad_maximum_fusion), channel_id=1, source_target_pairs={{0,96},{16,48},{32,0},{48,80},{64,32},{80,112},{96,64},{112,16},{1... | collective-permute-start | bytes 7077896 | tf_op jit(solution)/shard_map/ppermute | solution.py:208
  37.8 27.1 %collective-permute-start.7 = (bf16[2,768,384]{2,1,0:T(8,128)(2,1)}, bf16[2,768,384]{2,1,0:T(8,128)(2,1)S(1)}, u32[]{:S(2)}, u32[]{:S(2)}) collective-permute-start(bf16[2,768,384]{2,1,0:T(8,128)(2,1)} %collective-permute-done.refs_2_.refs_3_), channel_id=1, source_target_pairs={{0,32},{16,112},{32,64},{48,16},{64,96},{80,48},{96,0},{112,80},{1... | collective-permute-start | bytes 3538952 | tf_op jit(solution)/shard_map/ppermute | solution.py:212
  37.8 13.1 %collective-permute-start.4 = (bf16[768,384]{1,0:T(8,128)(2,1)S(1)}, bf16[768,384]{1,0:T(8,128)(2,1)S(1)}, u32[]{:S(2)}, u32[]{:S(2)}) collective-permute-start(bf16[768,384]{1,0:T(8,128)(2,1)S(1)} %get-tuple-element.63), channel_id=1, source_target_pairs={{0,16},{16,0},{32,48},{48,32},{64,80},{80,64},{96,112},{112,96},{1... | collective-permute-start | bytes 1769480 | tf_op jit(solution)/shard_map/ppermute | solution.py:210
  39.1 28.5 %collective-permute-start.5 = (bf16[2,768,384]{2,1,0:T(8,128)(2,1)}, bf16[2,768,384]{2,1,0:T(8,128)(2,1)S(1)}, u32[]{:S(2)}, u32[]{:S(2)}) collective-permute-start(bf16[2,768,384]{2,1,0:T(8,128)(2,1)} %collective-permute-done.refs_2_.refs_3_), channel_id=1, source_target_pairs={{0,4},{4,8},{8,12},{12,0},{1,5},{5,9},{9,13},{13,1},{2,6},{6,10},{... | collective-permute-start | bytes 3538952 | tf_op jit(solution)/shard_map/ppermute | solution.py:177
  40.1 27.6 %collective-permute-start.6 = (bf16[2,768,384]{2,1,0:T(8,128)(2,1)}, bf16[2,768,384]{2,1,0:T(8,128)(2,1)S(1)}, u32[]{:S(2)}, u32[]{:S(2)}) collective-permute-start(bf16[2,768,384]{2,1,0:T(8,128)(2,1)} %collective-permute-done.refs_2_.refs_3_), channel_id=1, source_target_pairs={{4,0},{8,4},{12,8},{0,12},{5,1},{9,5},{13,9},{1,13},{6,2},{10,6},{... | collective-permute-start | bytes 3538952 | tf_op jit(solution)/shard_map/ppermute | solution.py:177
  64.9 32.2 %collective-permute-start.11 = (bf16[2,768,384]{2,1,0:T(8,128)(2,1)S(1)}, bf16[2,768,384]{2,1,0:T(8,128)(2,1)S(1)}, u32[]{:S(2)}, u32[]{:S(2)}) collective-permute-start(bf16[2,768,384]{2,1,0:T(8,128)(2,1)S(1)} %collective-permute-done.7.refs_4_), channel_id=1, source_target_pairs={{0,4},{4,8},{8,12},{12,0},{1,5},{5,9},{9,13},{13,1},{2,6},{6,10},{... | collective-permute-start | bytes 3538952 | tf_op jit(solution)/shard_map/ppermute | solution.py:177
  65.5 31.7 %collective-permute-start.12 = (bf16[2,768,384]{2,1,0:T(8,128)(2,1)S(1)}, bf16[2,768,384]{2,1,0:T(8,128)(2,1)S(1)}, u32[]{:S(2)}, u32[]{:S(2)}) collective-permute-start(bf16[2,768,384]{2,1,0:T(8,128)(2,1)S(1)} %collective-permute-done.7.refs_4_), channel_id=1, source_target_pairs={{4,0},{8,4},{12,8},{0,12},{5,1},{9,5},{13,9},{1,13},{6,2},{10,6},{... | collective-permute-start | bytes 3538952 | tf_op jit(solution)/shard_map/ppermute | solution.py:177
  90.7 12.3 %collective-permute-start.9 = (bf16[384,384]{1,0:T(8,128)(2,1)S(1)}, bf16[384,384]{1,0:T(8,128)(2,1)S(1)}, u32[]{:S(2)}, u32[]{:S(2)}) collective-permute-start(bf16[384,384]{1,0:T(8,128)(2,1)S(1)} %shard_map.42), channel_id=1, source_target_pairs={{0,16},{16,0},{32,48},{48,32},{64,80},{80,64},{96,112},{112,96},{1... | collective-permute-start | bytes 884744 | tf_op jit(solution)/shard_map/ppermute | solution.py:229
  96.8 7.9 %collective-permute-start.10 = (bf16[384,384]{1,0:T(8,128)(2,1)S(1)}, bf16[384,384]{1,0:T(8,128)(2,1)S(1)}, u32[]{:S(2)}, u32[]{:S(2)}) collective-permute-start(bf16[384,384]{1,0:T(8,128)(2,1)S(1)} %shard_map.43), channel_id=1, source_target_pairs={{0,16},{16,0},{32,48},{48,32},{64,80},{80,64},{96,112},{112,96},{1... | collective-permute-start | bytes 884744 | tf_op jit(solution)/shard_map/ppermute | solution.py:229
  105.4 5.1 %collective-permute-start.16 = (bf16[384,768]{1,0:T(8,128)(2,1)S(1)}, bf16[384,768]{1,0:T(8,128)(2,1)S(1)}, u32[]{:S(2)}, u32[]{:S(2)}) collective-permute-start(bf16[384,768]{1,0:T(8,128)(2,1)S(1)} %convolution_convert_fusion.1), channel_id=1, source_target_pairs={{0,1},{1,0},{2,3},{3,2},{4,5},{5,4},{6,7},{7,6},{8,9},{9,8},{10,11... | collective-permute-start | bytes 1769480 | tf_op jit(solution)/shard_map/ppermute | solution.py:244
  108.7 4.9 %collective-permute-start.14 = (bf16[384,768]{1,0:T(8,128)(2,1)S(1)}, bf16[384,768]{1,0:T(8,128)(2,1)S(1)}, u32[]{:S(2)}, u32[]{:S(2)}) collective-permute-start(bf16[384,768]{1,0:T(8,128)(2,1)S(1)} %convolution_convert_fusion.2), channel_id=1, source_target_pairs={{0,1},{1,0},{2,3},{3,2},{4,5},{5,4},{6,7},{7,6},{8,9},{9,8},{10,11... | collective-permute-start | bytes 1769480 | tf_op jit(solution)/shard_map/ppermute | solution.py:244
  109.9 30.4 %collective-permute-start.13 = (bf16[768,768]{1,0:T(8,128)(2,1)S(1)}, bf16[768,768]{1,0:T(8,128)(2,1)S(1)}, u32[]{:S(2)}, u32[]{:S(2)}) collective-permute-start(bf16[768,768]{1,0:T(8,128)(2,1)S(1)} %convolution_convert_fusion), channel_id=1, source_target_pairs={{0,1},{1,0},{2,3},{3,2},{4,5},{5,4},{6,7},{7,6},{8,9},{9,8},{10,11... | collective-permute-start | bytes 3538952 | tf_op jit(solution)/shard_map/ppermute | solution.py:247
  111.1 16.5 %collective-permute-start.17 = (bf16[384,768]{1,0:T(8,128)(2,1)S(1)}, bf16[384,768]{1,0:T(8,128)(2,1)S(1)}, u32[]{:S(2)}, u32[]{:S(2)}) collective-permute-start(bf16[384,768]{1,0:T(8,128)(2,1)S(1)} %add_convert_fusion.1), channel_id=1, source_target_pairs={{0,2},{1,3},{2,0},{3,1},{4,6},{5,7},{6,4},{7,5},{8,10},{9,11},{10,... | collective-permute-start | bytes 1769480 | tf_op jit(solution)/shard_map/ppermute | solution.py:246
  114.3 26.0 %collective-permute-start.15 = (bf16[384,768]{1,0:T(8,128)(2,1)S(1)}, bf16[384,768]{1,0:T(8,128)(2,1)S(1)}, u32[]{:S(2)}, u32[]{:S(2)}) collective-permute-start(bf16[384,768]{1,0:T(8,128)(2,1)S(1)} %add_convert_fusion.2), channel_id=1, source_target_pairs={{0,2},{1,3},{2,0},{3,1},{4,6},{5,7},{6,4},{7,5},{8,10},{9,11},{10,... | collective-permute-start | bytes 1769480 | tf_op jit(solution)/shard_map/ppermute | solution.py:246
where the time goes:
time: 143 us; the launch traced here: 142 us
  Pallas kernels  52.3 us (37%)
  waiting for transfers between devices  48 us (34%)
  starting transfers between devices  27 us (19%)
  local copies, waits for them, and re-layouts  6.3 us (4%)
  matrix products  5.78 us (4%)
  other arithmetic  2.8 us (2%)
    pallas_call x8, Pallas kernels, attend(): pl.pallas_call(functools.partial(attend_kernel, tuple(gates), state is No...  52.3 us
    ppermute x2, waiting for transfers between devices, body(): fars.append(lax.ppermute(away, 'ta', hi_pairs))  25.4 us
    ppermute x3, waiting for transfers between devices, above_below(): lax.ppermute(cells, 'wa', down_pairs)  13.4 us
    dot_general x6, matrix products, partial_of(): jnp.dot(attention[start:stop], weights[group], preferred_element_type=jnp...  5.78 us
    ppermute x3, starting transfers between devices, above_below(): lax.ppermute(cells, 'wa', up_pairs)  5.39 us
    ppermute x1, waiting for transfers between devices, body(): far_p_rows = lax.ppermute(jnp.stack([own_up, own_down]), 'ha', native_pairs)  5.34 us
    ppermute x1, starting transfers between devices, body(): far_p = lax.ppermute(kv_own, 'ha', native_pairs)  3.76 us
    ppermute x1, starting transfers between devices, body(): far_p_rows = lax.ppermute(jnp.stack([own_up, own_down]), 'ha', native_pairs)  3.73 us
  transfers between devices with their start and end apart: 18, of which 7 were waited for; matrix products, arithmetic and copies ran while one was open for 6% of the time, Pallas kernels for 37%

commit v1 on v0

--- a/solution.py
+++ b/solution.py
@@ -246,6 +246,7 @@
         fars.append(lax.ppermute(away, "ta", hi_pairs))
     home_taken = lax.ppermute(partial_of(2, 0, tokens).astype(jnp.bfloat16), "ta", core_pairs)
     home = partial_of(3, 0, tokens) + home_taken.astype(jnp.float32)
+    home, *fars = lax.optimization_barrier((home, *fars))
     result = home + jnp.concatenate(fars, axis=0).astype(jnp.float32)
     return result.astype(jnp.bfloat16).reshape(frames, rows, cols, width)
 

time: 143 us -> 141 us (0.986)
  waiting for transfers between devices: 48 us -> 45.7 us
    ppermute x2, waiting for transfers between devices: 25.4 us -> 23 us  [body(): fars.append(lax.ppermute(away, 'ta', hi_pairs))]
    another operation x1, other arithmetic: 1.89 us -> 0.27 us  [body(): far_p_rows = lax.ppermute(jnp.stack([own_up, own_down]), 'ha', native_pairs)]
    unnamed x4 -> x6, local copies, waits for them, and re-layouts: 2.12 us -> 2.87 us
  transfers between devices with their start and end apart: 18 -> 18, of which waited for: 7 -> 8; matrix products, arithmetic and copies ran while one was open for 6% -> 6% of each run, Pallas kernels for 37% -> 37%
where the time goes in v1:
time: 141 us
  Pallas kernels  52.1 us (37%)
  waiting for transfers between devices  45.7 us (32%)
  starting transfers between devices  28.4 us (20%)
  local copies, waits for them, and re-layouts  7.05 us (5%)
  matrix products  4.69 us (3%)
  other arithmetic  2.52 us (2%)
    pallas_call x8, Pallas kernels, attend(): pl.pallas_call(functools.partial(attend_kernel, tuple(gates), state is No...  52.1 us
    ppermute x2, waiting for transfers between devices, body(): fars.append(lax.ppermute(away, 'ta', hi_pairs))  23 us
    ppermute x3, waiting for transfers between devices, above_below(): lax.ppermute(cells, 'wa', down_pairs)  13.3 us
    ppermute x3, starting transfers between devices, above_below(): lax.ppermute(cells, 'wa', up_pairs)  6.12 us
    ppermute x1, waiting for transfers between devices, body(): far_p_rows = lax.ppermute(jnp.stack([own_up, own_down]), 'ha', native_pairs)  5.38 us
    dot_general x6, matrix products, partial_of(): jnp.dot(attention[start:stop], weights[group], preferred_element_type=jnp...  4.69 us
    ppermute x2, starting transfers between devices, body(): fars.append(lax.ppermute(away, 'ta', hi_pairs))  4.36 us
    ppermute x1, starting transfers between devices, body(): far_p_rows = lax.ppermute(jnp.stack([own_up, own_down]), 'ha', native_pairs)  3.84 us
  transfers between devices with their start and end apart: 18, of which 8 were waited for; matrix products, arithmetic and copies ran while one was open for 6% of the time, Pallas kernels for 37%

profile of v1, /device:TPU:1, one launch (start us, length us, event | category | flops | bytes accessed | tf_op | source)
XLA Modules:
  0.0 140.6 jit_solution(11757313585086808799)
XLA Ops:
  0.0 1.7 %copy-done = bf16[2,12,8,8,768]{4,3,2,1,0:T(8,128)(2,1)S(1)} copy-done((bf16[2,12,8,8,768]{4,3,2,1,0:T(8,128)(2,1)S(1)}, bf16[2,12,8,8,768]{4,3,2,1,0:T(8,128)(2,1)}, u32[]{:S(2)}) %copy-start) | copy-done | bytes 2359320
  1.7 1.1 constant_dynamic-slice_fusion.5
  2.9 2.2 %collective-permute-start.1 = (bf16[2,768,384]{2,1,0:T(8,128)(2,1)S(1)}, bf16[2,768,384]{2,1,0:T(8,128)(2,1)S(1)}, u32[]{:S(2)}, u32[]{:S(2)}) collective-permute-start(bf16[2,768,384]{2,1,0:T(8,128)(2,1)S(1)} %constant_dynamic-slice_fusion.3.refs_2_), channel_id=1, source_target_pairs={{0,4},{4,8},{8,12},{12,0},{1,5},{5,9},{9,13},{13,1},{2,6},{6,10},{... | collective-permute-start | bytes 3538952 | tf_op jit(solution)/shard_map/ppermute | solution.py:177
  5.1 1.5 %collective-permute-start.2 = (bf16[2,768,384]{2,1,0:T(8,128)(2,1)S(1)}, bf16[2,768,384]{2,1,0:T(8,128)(2,1)S(1)}, u32[]{:S(2)}, u32[]{:S(2)}) collective-permute-start(bf16[2,768,384]{2,1,0:T(8,128)(2,1)S(1)} %constant_dynamic-slice_fusion.3.refs_2_), channel_id=1, source_target_pairs={{4,0},{8,4},{12,8},{0,12},{5,1},{9,5},{13,9},{1,13},{6,2},{10,6},{... | collective-permute-start | bytes 3538952 | tf_op jit(solution)/shard_map/ppermute | solution.py:177
  6.6 3.8 %collective-permute-start.3 = (bf16[2,768,384]{2,1,0:T(8,128)(2,1)S(1)}, bf16[2,768,384]{2,1,0:T(8,128)(2,1)}, u32[]{:S(2)}, u32[]{:S(2)}) collective-permute-start(bf16[2,768,384]{2,1,0:T(8,128)(2,1)S(1)} %constant_dynamic-slice_fusion.3.refs_2_), channel_id=1, source_target_pairs={{0,96},{16,48},{32,0},{48,80},{64,32},{80,112},{96,64},{112,16},{1... | collective-permute-start | bytes 3538952 | tf_op jit(solution)/shard_map/ppermute | solution.py:204
  10.5 2.7 %constant_dynamic-slice_fusion.1 = (bf16[384,3072]{1,0:T(8,128)(2,1)S(1)}, bf16[384,3072]{1,0:T(8,128)(2,1)S(1)}) fusion(bf16[768,3072]{1,0:T(8,128)(2,1)} %param.5, s32[]{:T(128)S(6)} %select_n.34, s32[]{:T(128)S(6)} %select_n.35), kind=kLoop, calls=%fused_computation.28 | loop fusion | bytes 9437192 | tf_op jit(solution)/shard_map/dynamic_slice | solution.py:197
  13.3 0.8 fusion
  14.6 4.1 %shard_map.37 = (f32[768,768]{1,0:T(8,128)S(1)}, f32[768,384]{1,0:T(8,128)S(1)}) custom-call(s32[8]{0:T(128)S(1)} %convert_element_type.33.refs_0_, bf16[768,384]{1,0:T(8,128)(2,1)S(1)} %get-tuple-element.119.refs_1_, bf16[2,768,384]{2,1,0:T(8,128)(2,1)S(1)} %constant_dynamic-slice_fusion.3.refs_2_), custom_call_target="tpu_custom_call" | custom-call | flops 56623104 | bytes 1024 | tf_op jit(solution)/shard_map/pallas_call | solution.py:147
  18.8 13.3 %collective-permute-done.1.refs_3_.refs_4_ = bf16[2,768,384]{2,1,0:T(8,128)(2,1)S(1)} collective-permute-done((bf16[2,768,384]{2,1,0:T(8,128)(2,1)S(1)}, bf16[2,768,384]{2,1,0:T(8,128)(2,1)S(1)}, u32[]{:S(2)}, u32[]{:S(2)}) %collective-permute-start.1) | collective-permute-done | bytes 1179680 | tf_op jit(solution)/shard_map/ppermute | solution.py:177
  32.4 3.8 %collective-permute-start.8 = (bf16[2,2,768,384]{3,2,1,0:T(8,128)(2,1)S(1)}, bf16[2,2,768,384]{3,2,1,0:T(8,128)(2,1)S(1)}, u32[]{:S(2)}, u32[]{:S(2)}) collective-permute-start(bf16[2,2,768,384]{3,2,1,0:T(8,128)(2,1)S(1)} %pad_maximum_fusion), channel_id=1, source_target_pairs={{0,96},{16,48},{32,0},{48,80},{64,32},{80,112},{96,64},{112,16},{1... | collective-permute-start | bytes 7077896 | tf_op jit(solution)/shard_map/ppermute | solution.py:208
  36.8 1.5 %collective-permute-start.4 = (bf16[768,384]{1,0:T(8,128)(2,1)S(1)}, bf16[768,384]{1,0:T(8,128)(2,1)S(1)}, u32[]{:S(2)}, u32[]{:S(2)}) collective-permute-start(bf16[768,384]{1,0:T(8,128)(2,1)S(1)} %get-tuple-element.66), channel_id=1, source_target_pairs={{0,16},{16,0},{32,48},{48,32},{64,80},{80,64},{96,112},{112,96},{1... | collective-permute-start | bytes 1769480 | tf_op jit(solution)/shard_map/ppermute | solution.py:210
  38.4 2.5 %collective-permute-start.6 = (bf16[2,768,384]{2,1,0:T(8,128)(2,1)}, bf16[2,768,384]{2,1,0:T(8,128)(2,1)S(1)}, u32[]{:S(2)}, u32[]{:S(2)}) collective-permute-start(bf16[2,768,384]{2,1,0:T(8,128)(2,1)} %collective-permute-done.refs_2_.refs_3_), channel_id=1, source_target_pairs={{4,0},{8,4},{12,8},{0,12},{5,1},{9,5},{13,9},{1,13},{6,2},{10,6},{... | collective-permute-start | bytes 3538952 | tf_op jit(solution)/shard_map/ppermute | solution.py:177
  41.0 8.0 %shard_map.38 = (f32[768,768]{1,0:T(8,128)S(1)}, f32[768,384]{1,0:T(8,128)S(1)}) custom-call(s32[8]{0:T(128)S(1)} %convert_element_type.33.refs_0_, bf16[768,384]{1,0:T(8,128)(2,1)S(1)} %get-tuple-element.119.refs_1_, bf16[2,768,384]{2,1,0:T(8,128)(2,1)} %collective-permute-done.refs_2_.refs_3_, ...), custom_call_target="tpu_custom_call" | custom-call | flops 169869312 | bytes 1024 | tf_op jit(solution)/shard_map/pallas_call | solution.py:147
  49.4 12.7 %shard_map.39 = (f32[768,768]{1,0:T(8,128)S(1)}, f32[768,384]{1,0:T(8,128)S(1)}) custom-call(s32[8]{0:T(128)S(1)} %convert_element_type.33.refs_0_, bf16[768,384]{1,0:T(8,128)(2,1)S(1)} %collective-permute-done.4.refs_1_, bf16[2,768,384]{2,1,0:T(8,128)(2,1)S(1)} %constant_dynamic-slice_fusion.3.refs_2_, ...), custom_call_target="tpu_custom_call" | custom-call | flops 283115520 | bytes 1024 | tf_op jit(solution)/shard_map/pallas_call | solution.py:147
  62.1 1.3 collective-permute-done.7.refs_4_
  64.0 2.1 %collective-permute-start.12 = (bf16[2,768,384]{2,1,0:T(8,128)(2,1)S(1)}, bf16[2,768,384]{2,1,0:T(8,128)(2,1)S(1)}, u32[]{:S(2)}, u32[]{:S(2)}) collective-permute-start(bf16[2,768,384]{2,1,0:T(8,128)(2,1)S(1)} %collective-permute-done.7.refs_4_), channel_id=1, source_target_pairs={{4,0},{8,4},{12,8},{0,12},{5,1},{9,5},{13,9},{1,13},{6,2},{10,6},{... | collective-permute-start | bytes 3538952 | tf_op jit(solution)/shard_map/ppermute | solution.py:177
  66.1 6.0 %shard_map.40 = (f32[768,768]{1,0:T(8,128)S(1)}, f32[768,384]{1,0:T(8,128)S(1)}) custom-call(s32[8]{0:T(128)S(1)} %convert_element_type.33.refs_0_, bf16[768,384]{1,0:T(8,128)(2,1)S(1)} %collective-permute-done.4.refs_1_, bf16[2,768,384]{2,1,0:T(8,128)(2,1)S(1)} %collective-permute-done.5.refs_2_, bf16[2,768,384]{2,1,0:T(8,128)(2,1)S(1)} %collective-permute-done.6.refs_3_, ...), custom_call_target="tpu_custom_call" | custom-call | flops 113246208 | bytes 1024 | tf_op jit(solution)/shard_map/pallas_call | solution.py:147
  72.0 7.9 %shard_map.41 = (f32[768,768]{1,0:T(8,128)S(1)}, f32[768,384]{1,0:T(8,128)S(1)}) custom-call(s32[8]{0:T(128)S(1)} %convert_element_type.33.refs_0_, bf16[768,384]{1,0:T(8,128)(2,1)S(1)} %get-tuple-element.119.refs_1_, bf16[2,768,384]{2,1,0:T(8,128)(2,1)S(1)} %collective-permute-done.5.refs_2_, bf16[2,768,384]{2,1,0:T(8,128)(2,1)S(1)} %collective-permute-done.6.refs_3_, ...), custom_call_target="tpu_custom_call" | custom-call | flops 169869312 | bytes 1024 | tf_op jit(solution)/shard_map/pallas_call | solution.py:147
  80.0 5.4 %collective-permute-done.8.refs_2_.refs_3_ = bf16[2,2,768,384]{3,2,1,0:T(8,128)(2,1)S(1)} collective-permute-done((bf16[2,2,768,384]{3,2,1,0:T(8,128)(2,1)S(1)}, bf16[2,2,768,384]{3,2,1,0:T(8,128)(2,1)S(1)}, u32[]{:S(2)}, u32[]{:S(2)}) %collective-permute-start.8) | collective-permute-done | bytes 2359328 | tf_op jit(solution)/shard_map/ppermute | solution.py:208
  85.4 3.8 %shard_map.42 = bf16[384,384]{1,0:T(8,128)(2,1)S(1)} custom-call(s32[8]{0:T(128)S(1)} %convert_element_type.33.refs_0_, bf16[768,384]{1,0:T(8,128)(2,1)S(1)} %collective-permute-done.4.refs_1_, bf16[2,2,768,384]{3,2,1,0:T(8,128)(2,1)S(1)} %collective-permute-done.8.refs_2_.refs_3_, bf16[2,2,768,384]{3,2,1,0:T(8,128)(2,1)S(1)} %collective-permute-done.8.refs_2_.refs_3_, ...), custom_call_target="tpu_custom_call" | custom-call | flops 56623104 | bytes 1024 | tf_op jit(solution)/shard_map/pallas_call | solution.py:147
  89.2 2.1 %collective-permute-start.9 = (bf16[384,384]{1,0:T(8,128)(2,1)S(1)}, bf16[384,384]{1,0:T(8,128)(2,1)S(1)}, u32[]{:S(2)}, u32[]{:S(2)}) collective-permute-start(bf16[384,384]{1,0:T(8,128)(2,1)S(1)} %shard_map.42), channel_id=1, source_target_pairs={{0,16},{16,0},{32,48},{48,32},{64,80},{80,64},{96,112},{112,96},{1... | collective-permute-start | bytes 884744 | tf_op jit(solution)/shard_map/ppermute | solution.py:229
  91.3 3.8 %shard_map.43 = bf16[384,384]{1,0:T(8,128)(2,1)S(1)} custom-call(s32[8]{0:T(128)S(1)} %convert_element_type.33.refs_0_, bf16[768,384]{1,0:T(8,128)(2,1)S(1)} %collective-permute-done.4.refs_1_, bf16[2,2,768,384]{3,2,1,0:T(8,128)(2,1)S(1)} %collective-permute-done.8.refs_2_.refs_3_, bf16[2,2,768,384]{3,2,1,0:T(8,128)(2,1)S(1)} %collective-permute-done.8.refs_2_.refs_3_, ...), custom_call_target="tpu_custom_call" | custom-call | flops 56623104 | bytes 1024 | tf_op jit(solution)/shard_map/pallas_call | solution.py:147
  95.4 5.8 %shard_map.44 = bf16[768,384]{1,0:T(8,128)(2,1)S(1)} custom-call(s32[8]{0:T(128)S(1)} %convert_element_type.33.refs_0_, bf16[768,384]{1,0:T(8,128)(2,1)S(1)} %get-tuple-element.119.refs_1_, bf16[2,768,384]{2,1,0:T(8,128)(2,1)S(1)} %collective-permute-done.11.refs_2_, bf16[2,768,384]{2,1,0:T(8,128)(2,1)S(1)} %collective-permute-done.12.refs_3_, ...), custom_call_target="tpu_custom_call" | custom-call | flops 113246208 | bytes 1024 | tf_op jit(solution)/shard_map/pallas_call | solution.py:147
  101.3 1.6 %collective-permute-done.10 = bf16[384,384]{1,0:T(8,128)(2,1)S(1)} collective-permute-done((bf16[384,384]{1,0:T(8,128)(2,1)S(1)}, bf16[384,384]{1,0:T(8,128)(2,1)S(1)}, u32[]{:S(2)}, u32[]{:S(2)}) %collective-permute-start.10) | collective-permute-done | bytes 294944 | tf_op jit(solution)/shard_map/ppermute | solution.py:229
  103.6 2.7 %collective-permute-start.14 = (bf16[384,768]{1,0:T(8,128)(2,1)S(1)}, bf16[384,768]{1,0:T(8,128)(2,1)S(1)}, u32[]{:S(2)}, u32[]{:S(2)}) collective-permute-start(bf16[384,768]{1,0:T(8,128)(2,1)S(1)} %convolution_convert_fusion.2), channel_id=1, source_target_pairs={{0,1},{1,0},{2,3},{3,2},{4,5},{5,4},{6,7},{7,6},{8,9},{9,8},{10,11... | collective-permute-start | bytes 1769480 | tf_op jit(solution)/shard_map/ppermute | solution.py:244
  106.4 1.1 convolution_convert_fusion
  109.4 2.5 %collective-permute-start.15 = (bf16[384,768]{1,0:T(8,128)(2,1)S(1)}, bf16[384,768]{1,0:T(8,128)(2,1)S(1)}, u32[]{:S(2)}, u32[]{:S(2)}) collective-permute-start(bf16[384,768]{1,0:T(8,128)(2,1)S(1)} %add_convert_fusion.2), channel_id=1, source_target_pairs={{0,2},{1,3},{2,0},{3,1},{4,6},{5,7},{6,4},{7,5},{8,10},{9,11},{10,... | collective-permute-start | bytes 1769480 | tf_op jit(solution)/shard_map/ppermute | solution.py:246
  112.6 1.8 %collective-permute-start.17 = (bf16[384,768]{1,0:T(8,128)(2,1)S(1)}, bf16[384,768]{1,0:T(8,128)(2,1)S(1)}, u32[]{:S(2)}, u32[]{:S(2)}) collective-permute-start(bf16[384,768]{1,0:T(8,128)(2,1)S(1)} %add_convert_fusion.1), channel_id=1, source_target_pairs={{0,2},{1,3},{2,0},{3,1},{4,6},{5,7},{6,4},{7,5},{8,10},{9,11},{10,... | collective-permute-start | bytes 1769480 | tf_op jit(solution)/shard_map/ppermute | solution.py:246
  114.4 1.1 convert_add_fusion
  115.5 10.4 %collective-permute-done.15 = bf16[384,768]{1,0:T(8,128)(2,1)S(1)} collective-permute-done((bf16[384,768]{1,0:T(8,128)(2,1)S(1)}, bf16[384,768]{1,0:T(8,128)(2,1)S(1)}, u32[]{:S(2)}, u32[]{:S(2)}) %collective-permute-start.15) | collective-permute-done | bytes 589856 | tf_op jit(solution)/shard_map/ppermute | solution.py:246
  125.9 12.6 %collective-permute-done.17 = bf16[384,768]{1,0:T(8,128)(2,1)S(1)} collective-permute-done((bf16[384,768]{1,0:T(8,128)(2,1)S(1)}, bf16[384,768]{1,0:T(8,128)(2,1)S(1)}, u32[]{:S(2)}, u32[]{:S(2)}) %collective-permute-start.17) | collective-permute-done | bytes 589856 | tf_op jit(solution)/shard_map/ppermute | solution.py:246
  138.6 1.3 add_convert_fusion
  (34 shorter events, 7.2 us)
Async XLA Ops:
  0.0 1.7 %copy-start = (bf16[2,12,8,8,768]{4,3,2,1,0:T(8,128)(2,1)S(1)}, bf16[2,12,8,8,768]{4,3,2,1,0:T(8,128)(2,1)}, u32[]{:S(2)}) copy-start(bf16[2,12,8,8,768]{4,3,2,1,0:T(8,128)(2,1)} %param.4) | copy-start | bytes 7077892
  2.9 29.2 %collective-permute-start.1 = (bf16[2,768,384]{2,1,0:T(8,128)(2,1)S(1)}, bf16[2,768,384]{2,1,0:T(8,128)(2,1)S(1)}, u32[]{:S(2)}, u32[]{:S(2)}) collective-permute-start(bf16[2,768,384]{2,1,0:T(8,128)(2,1)S(1)} %constant_dynamic-slice_fusion.3.refs_2_), channel_id=1, source_target_pairs={{0,4},{4,8},{8,12},{12,0},{1,5},{5,9},{9,13},{13,1},{2,6},{6,10},{... | collective-permute-start | bytes 3538952 | tf_op jit(solution)/shard_map/ppermute | solution.py:177
  5.1 27.0 %collective-permute-start.2 = (bf16[2,768,384]{2,1,0:T(8,128)(2,1)S(1)}, bf16[2,768,384]{2,1,0:T(8,128)(2,1)S(1)}, u32[]{:S(2)}, u32[]{:S(2)}) collective-permute-start(bf16[2,768,384]{2,1,0:T(8,128)(2,1)S(1)} %constant_dynamic-slice_fusion.3.refs_2_), channel_id=1, source_target_pairs={{4,0},{8,4},{12,8},{0,12},{5,1},{9,5},{13,9},{1,13},{6,2},{10,6},{... | collective-permute-start | bytes 3538952 | tf_op jit(solution)/shard_map/ppermute | solution.py:177
  6.6 30.2 %collective-permute-start.3 = (bf16[2,768,384]{2,1,0:T(8,128)(2,1)S(1)}, bf16[2,768,384]{2,1,0:T(8,128)(2,1)}, u32[]{:S(2)}, u32[]{:S(2)}) collective-permute-start(bf16[2,768,384]{2,1,0:T(8,128)(2,1)S(1)} %constant_dynamic-slice_fusion.3.refs_2_), channel_id=1, source_target_pairs={{0,96},{16,48},{32,0},{48,80},{64,32},{80,112},{96,64},{112,16},{1... | collective-permute-start | bytes 3538952 | tf_op jit(solution)/shard_map/ppermute | solution.py:204
  10.4 26.4 %collective-permute-start = (bf16[2,768,384]{2,1,0:T(8,128)(2,1)}, bf16[2,768,384]{2,1,0:T(8,128)(2,1)}, u32[]{:S(2)}, u32[]{:S(2)}) collective-permute-start(bf16[2,768,384]{2,1,0:T(8,128)(2,1)} %constant_dynamic-slice_fusion.5), channel_id=1, source_target_pairs={{0,16},{16,0},{32,48},{48,32},{64,80},{80,64},{96,112},{112,96},{1... | collective-permute-start | bytes 3538952 | tf_op jit(solution)/shard_map/ppermute | solution.py:202
  13.2 1.3 copy-start.2
  32.4 53.0 %collective-permute-start.8 = (bf16[2,2,768,384]{3,2,1,0:T(8,128)(2,1)S(1)}, bf16[2,2,768,384]{3,2,1,0:T(8,128)(2,1)S(1)}, u32[]{:S(2)}, u32[]{:S(2)}) collective-permute-start(bf16[2,2,768,384]{3,2,1,0:T(8,128)(2,1)S(1)} %pad_maximum_fusion), channel_id=1, source_target_pairs={{0,96},{16,48},{32,0},{48,80},{64,32},{80,112},{96,64},{112,16},{1... | collective-permute-start | bytes 7077896 | tf_op jit(solution)/shard_map/ppermute | solution.py:208
  36.8 26.6 %collective-permute-start.7 = (bf16[2,768,384]{2,1,0:T(8,128)(2,1)}, bf16[2,768,384]{2,1,0:T(8,128)(2,1)S(1)}, u32[]{:S(2)}, u32[]{:S(2)}) collective-permute-start(bf16[2,768,384]{2,1,0:T(8,128)(2,1)} %collective-permute-done.refs_2_.refs_3_), channel_id=1, source_target_pairs={{0,32},{16,112},{32,64},{48,16},{64,96},{80,48},{96,0},{112,80},{1... | collective-permute-start | bytes 3538952 | tf_op jit(solution)/shard_map/ppermute | solution.py:212
  36.8 12.6 %collective-permute-start.4 = (bf16[768,384]{1,0:T(8,128)(2,1)S(1)}, bf16[768,384]{1,0:T(8,128)(2,1)S(1)}, u32[]{:S(2)}, u32[]{:S(2)}) collective-permute-start(bf16[768,384]{1,0:T(8,128)(2,1)S(1)} %get-tuple-element.66), channel_id=1, source_target_pairs={{0,16},{16,0},{32,48},{48,32},{64,80},{80,64},{96,112},{112,96},{1... | collective-permute-start | bytes 1769480 | tf_op jit(solution)/shard_map/ppermute | solution.py:210
  38.3 27.8 %collective-permute-start.5 = (bf16[2,768,384]{2,1,0:T(8,128)(2,1)}, bf16[2,768,384]{2,1,0:T(8,128)(2,1)S(1)}, u32[]{:S(2)}, u32[]{:S(2)}) collective-permute-start(bf16[2,768,384]{2,1,0:T(8,128)(2,1)} %collective-permute-done.refs_2_.refs_3_), channel_id=1, source_target_pairs={{0,4},{4,8},{8,12},{12,0},{1,5},{5,9},{9,13},{13,1},{2,6},{6,10},{... | collective-permute-start | bytes 3538952 | tf_op jit(solution)/shard_map/ppermute | solution.py:177
  38.4 27.6 %collective-permute-start.6 = (bf16[2,768,384]{2,1,0:T(8,128)(2,1)}, bf16[2,768,384]{2,1,0:T(8,128)(2,1)S(1)}, u32[]{:S(2)}, u32[]{:S(2)}) collective-permute-start(bf16[2,768,384]{2,1,0:T(8,128)(2,1)} %collective-permute-done.refs_2_.refs_3_), channel_id=1, source_target_pairs={{4,0},{8,4},{12,8},{0,12},{5,1},{9,5},{13,9},{1,13},{6,2},{10,6},{... | collective-permute-start | bytes 3538952 | tf_op jit(solution)/shard_map/ppermute | solution.py:177
  63.4 32.1 %collective-permute-start.11 = (bf16[2,768,384]{2,1,0:T(8,128)(2,1)S(1)}, bf16[2,768,384]{2,1,0:T(8,128)(2,1)S(1)}, u32[]{:S(2)}, u32[]{:S(2)}) collective-permute-start(bf16[2,768,384]{2,1,0:T(8,128)(2,1)S(1)} %collective-permute-done.7.refs_4_), channel_id=1, source_target_pairs={{0,4},{4,8},{8,12},{12,0},{1,5},{5,9},{9,13},{13,1},{2,6},{6,10},{... | collective-permute-start | bytes 3538952 | tf_op jit(solution)/shard_map/ppermute | solution.py:177
  64.0 31.5 %collective-permute-start.12 = (bf16[2,768,384]{2,1,0:T(8,128)(2,1)S(1)}, bf16[2,768,384]{2,1,0:T(8,128)(2,1)S(1)}, u32[]{:S(2)}, u32[]{:S(2)}) collective-permute-start(bf16[2,768,384]{2,1,0:T(8,128)(2,1)S(1)} %collective-permute-done.7.refs_4_), channel_id=1, source_target_pairs={{4,0},{8,4},{12,8},{0,12},{5,1},{9,5},{13,9},{1,13},{6,2},{10,6},{... | collective-permute-start | bytes 3538952 | tf_op jit(solution)/shard_map/ppermute | solution.py:177
  89.2 12.1 %collective-permute-start.9 = (bf16[384,384]{1,0:T(8,128)(2,1)S(1)}, bf16[384,384]{1,0:T(8,128)(2,1)S(1)}, u32[]{:S(2)}, u32[]{:S(2)}) collective-permute-start(bf16[384,384]{1,0:T(8,128)(2,1)S(1)} %shard_map.42), channel_id=1, source_target_pairs={{0,16},{16,0},{32,48},{48,32},{64,80},{80,64},{96,112},{112,96},{1... | collective-permute-start | bytes 884744 | tf_op jit(solution)/shard_map/ppermute | solution.py:229
  95.1 7.8 %collective-permute-start.10 = (bf16[384,384]{1,0:T(8,128)(2,1)S(1)}, bf16[384,384]{1,0:T(8,128)(2,1)S(1)}, u32[]{:S(2)}, u32[]{:S(2)}) collective-permute-start(bf16[384,384]{1,0:T(8,128)(2,1)S(1)} %shard_map.43), channel_id=1, source_target_pairs={{0,16},{16,0},{32,48},{48,32},{64,80},{80,64},{96,112},{112,96},{1... | collective-permute-start | bytes 884744 | tf_op jit(solution)/shard_map/ppermute | solution.py:229
  103.6 5.1 %collective-permute-start.14 = (bf16[384,768]{1,0:T(8,128)(2,1)S(1)}, bf16[384,768]{1,0:T(8,128)(2,1)S(1)}, u32[]{:S(2)}, u32[]{:S(2)}) collective-permute-start(bf16[384,768]{1,0:T(8,128)(2,1)S(1)} %convolution_convert_fusion.2), channel_id=1, source_target_pairs={{0,1},{1,0},{2,3},{3,2},{4,5},{5,4},{6,7},{7,6},{8,9},{9,8},{10,11... | collective-permute-start | bytes 1769480 | tf_op jit(solution)/shard_map/ppermute | solution.py:244
  107.4 6.9 %collective-permute-start.13 = (bf16[768,768]{1,0:T(8,128)(2,1)S(1)}, bf16[768,768]{1,0:T(8,128)(2,1)S(1)}, u32[]{:S(2)}, u32[]{:S(2)}) collective-permute-start(bf16[768,768]{1,0:T(8,128)(2,1)S(1)} %convolution_convert_fusion), channel_id=1, source_target_pairs={{0,1},{1,0},{2,3},{3,2},{4,5},{5,4},{6,7},{7,6},{8,9},{9,8},{10,11... | collective-permute-start | bytes 3538952 | tf_op jit(solution)/shard_map/ppermute | solution.py:247
  108.2 3.7 %collective-permute-start.16 = (bf16[384,768]{1,0:T(8,128)(2,1)S(1)}, bf16[384,768]{1,0:T(8,128)(2,1)S(1)}, u32[]{:S(2)}, u32[]{:S(2)}) collective-permute-start(bf16[384,768]{1,0:T(8,128)(2,1)S(1)} %convolution_convert_fusion.1), channel_id=1, source_target_pairs={{0,1},{1,0},{2,3},{3,2},{4,5},{5,4},{6,7},{7,6},{8,9},{9,8},{10,11... | collective-permute-start | bytes 1769480 | tf_op jit(solution)/shard_map/ppermute | solution.py:244
  109.4 16.5 %collective-permute-start.15 = (bf16[384,768]{1,0:T(8,128)(2,1)S(1)}, bf16[384,768]{1,0:T(8,128)(2,1)S(1)}, u32[]{:S(2)}, u32[]{:S(2)}) collective-permute-start(bf16[384,768]{1,0:T(8,128)(2,1)S(1)} %add_convert_fusion.2), channel_id=1, source_target_pairs={{0,2},{1,3},{2,0},{3,1},{4,6},{5,7},{6,4},{7,5},{8,10},{9,11},{10,... | collective-permute-start | bytes 1769480 | tf_op jit(solution)/shard_map/ppermute | solution.py:246
  112.6 26.0 %collective-permute-start.17 = (bf16[384,768]{1,0:T(8,128)(2,1)S(1)}, bf16[384,768]{1,0:T(8,128)(2,1)S(1)}, u32[]{:S(2)}, u32[]{:S(2)}) collective-permute-start(bf16[384,768]{1,0:T(8,128)(2,1)S(1)} %add_convert_fusion.1), channel_id=1, source_target_pairs={{0,2},{1,3},{2,0},{3,1},{4,6},{5,7},{6,4},{7,5},{8,10},{9,11},{10,... | collective-permute-start | bytes 1769480 | tf_op jit(solution)/shard_map/ppermute | solution.py:246
  138.5 2.1 %copy-start.1 = (bf16[2,12,8,8,768]{4,3,2,1,0:T(8,128)(2,1)S(1)}, bf16[2,12,8,8,768]{4,3,2,1,0:T(8,128)(2,1)}, u32[]{:S(2)}) copy-start(bf16[2,12,8,8,768]{4,3,2,1,0:T(8,128)(2,1)} %param.4) | copy-start | bytes 7077892

commit v2 on v1

--- a/solution.py
+++ b/solution.py
@@ -150,7 +150,7 @@
         grid=(heads,),
         in_specs=in_specs,
         out_specs=out_specs,
-        compiler_params=pltpu.CompilerParams(vmem_limit_bytes=28 * 1024 * 1024),
+        compiler_params=pltpu.CompilerParams(vmem_limit_bytes=22 * 1024 * 1024),
         cost_estimate=pl.CostEstimate(flops=pairs * cost, bytes_accessed=1024, transcendentals=0),
     )(*args)
 

time: 141 us -> 141 us (level)
  no operation moved by 1% of the time
where the time goes in v2:
time: 141 us
  Pallas kernels  52.1 us (37%)
  waiting for transfers between devices  45.7 us (32%)
  starting transfers between devices  28.4 us (20%)
  local copies, waits for them, and re-layouts  7.05 us (5%)
  matrix products  4.69 us (3%)
  other arithmetic  2.52 us (2%)
    pallas_call x8, Pallas kernels, attend(): pl.pallas_call(functools.partial(attend_kernel, tuple(gates), state is No...  52.1 us
    ppermute x2, waiting for transfers between devices, body(): fars.append(lax.ppermute(away, 'ta', hi_pairs))  23 us
    ppermute x3, waiting for transfers between devices, above_below(): lax.ppermute(cells, 'wa', down_pairs)  13.3 us
    ppermute x3, starting transfers between devices, above_below(): lax.ppermute(cells, 'wa', up_pairs)  6.12 us
    ppermute x1, waiting for transfers between devices, body(): far_p_rows = lax.ppermute(jnp.stack([own_up, own_down]), 'ha', native_pairs)  5.38 us
    dot_general x6, matrix products, partial_of(): jnp.dot(attention[start:stop], weights[group], preferred_element_type=jnp...  4.69 us
    ppermute x2, starting transfers between devices, body(): fars.append(lax.ppermute(away, 'ta', hi_pairs))  4.36 us
    ppermute x1, starting transfers between devices, body(): far_p_rows = lax.ppermute(jnp.stack([own_up, own_down]), 'ha', native_pairs)  3.84 us
  transfers between devices with their start and end apart: 18, of which 8 were waited for; matrix products, arithmetic and copies ran while one was open for 6% of the time, Pallas kernels for 37%

profile of v2, /device:TPU:1, one launch (start us, length us, event | category | flops | bytes accessed | tf_op | source)
XLA Modules:
  0.0 140.6 jit_solution(7331327050567867431)
XLA Ops:
  0.0 1.7 %copy-done = bf16[2,12,8,8,768]{4,3,2,1,0:T(8,128)(2,1)S(1)} copy-done((bf16[2,12,8,8,768]{4,3,2,1,0:T(8,128)(2,1)S(1)}, bf16[2,12,8,8,768]{4,3,2,1,0:T(8,128)(2,1)}, u32[]{:S(2)}) %copy-start) | copy-done | bytes 2359320
  1.7 1.1 constant_dynamic-slice_fusion.5
  2.9 2.2 %collective-permute-start.1 = (bf16[2,768,384]{2,1,0:T(8,128)(2,1)S(1)}, bf16[2,768,384]{2,1,0:T(8,128)(2,1)S(1)}, u32[]{:S(2)}, u32[]{:S(2)}) collective-permute-start(bf16[2,768,384]{2,1,0:T(8,128)(2,1)S(1)} %constant_dynamic-slice_fusion.3.refs_2_), channel_id=1, source_target_pairs={{0,4},{4,8},{8,12},{12,0},{1,5},{5,9},{9,13},{13,1},{2,6},{6,10},{... | collective-permute-start | bytes 3538952 | tf_op jit(solution)/shard_map/ppermute | solution.py:177
  5.1 1.5 %collective-permute-start.2 = (bf16[2,768,384]{2,1,0:T(8,128)(2,1)S(1)}, bf16[2,768,384]{2,1,0:T(8,128)(2,1)S(1)}, u32[]{:S(2)}, u32[]{:S(2)}) collective-permute-start(bf16[2,768,384]{2,1,0:T(8,128)(2,1)S(1)} %constant_dynamic-slice_fusion.3.refs_2_), channel_id=1, source_target_pairs={{4,0},{8,4},{12,8},{0,12},{5,1},{9,5},{13,9},{1,13},{6,2},{10,6},{... | collective-permute-start | bytes 3538952 | tf_op jit(solution)/shard_map/ppermute | solution.py:177
  6.6 3.8 %collective-permute-start.3 = (bf16[2,768,384]{2,1,0:T(8,128)(2,1)S(1)}, bf16[2,768,384]{2,1,0:T(8,128)(2,1)}, u32[]{:S(2)}, u32[]{:S(2)}) collective-permute-start(bf16[2,768,384]{2,1,0:T(8,128)(2,1)S(1)} %constant_dynamic-slice_fusion.3.refs_2_), channel_id=1, source_target_pairs={{0,96},{16,48},{32,0},{48,80},{64,32},{80,112},{96,64},{112,16},{1... | collective-permute-start | bytes 3538952 | tf_op jit(solution)/shard_map/ppermute | solution.py:204
  10.5 2.7 %constant_dynamic-slice_fusion.1 = (bf16[384,3072]{1,0:T(8,128)(2,1)S(1)}, bf16[384,3072]{1,0:T(8,128)(2,1)S(1)}) fusion(bf16[768,3072]{1,0:T(8,128)(2,1)} %param.5, s32[]{:T(128)S(6)} %select_n.34, s32[]{:T(128)S(6)} %select_n.35), kind=kLoop, calls=%fused_computation.28 | loop fusion | bytes 9437192 | tf_op jit(solution)/shard_map/dynamic_slice | solution.py:197
  13.3 0.8 fusion
  14.6 4.1 %shard_map.37 = (f32[768,768]{1,0:T(8,128)S(1)}, f32[768,384]{1,0:T(8,128)S(1)}) custom-call(s32[8]{0:T(128)S(1)} %convert_element_type.33.refs_0_, bf16[768,384]{1,0:T(8,128)(2,1)S(1)} %get-tuple-element.119.refs_1_, bf16[2,768,384]{2,1,0:T(8,128)(2,1)S(1)} %constant_dynamic-slice_fusion.3.refs_2_), custom_call_target="tpu_custom_call" | custom-call | flops 56623104 | bytes 1024 | tf_op jit(solution)/shard_map/pallas_call | solution.py:147
  18.8 13.3 %collective-permute-done.1.refs_3_.refs_4_ = bf16[2,768,384]{2,1,0:T(8,128)(2,1)S(1)} collective-permute-done((bf16[2,768,384]{2,1,0:T(8,128)(2,1)S(1)}, bf16[2,768,384]{2,1,0:T(8,128)(2,1)S(1)}, u32[]{:S(2)}, u32[]{:S(2)}) %collective-permute-start.1) | collective-permute-done | bytes 1179680 | tf_op jit(solution)/shard_map/ppermute | solution.py:177
  32.4 3.8 %collective-permute-start.8 = (bf16[2,2,768,384]{3,2,1,0:T(8,128)(2,1)S(1)}, bf16[2,2,768,384]{3,2,1,0:T(8,128)(2,1)S(1)}, u32[]{:S(2)}, u32[]{:S(2)}) collective-permute-start(bf16[2,2,768,384]{3,2,1,0:T(8,128)(2,1)S(1)} %pad_maximum_fusion), channel_id=1, source_target_pairs={{0,96},{16,48},{32,0},{48,80},{64,32},{80,112},{96,64},{112,16},{1... | collective-permute-start | bytes 7077896 | tf_op jit(solution)/shard_map/ppermute | solution.py:208
  36.8 1.5 %collective-permute-start.4 = (bf16[768,384]{1,0:T(8,128)(2,1)S(1)}, bf16[768,384]{1,0:T(8,128)(2,1)S(1)}, u32[]{:S(2)}, u32[]{:S(2)}) collective-permute-start(bf16[768,384]{1,0:T(8,128)(2,1)S(1)} %get-tuple-element.66), channel_id=1, source_target_pairs={{0,16},{16,0},{32,48},{48,32},{64,80},{80,64},{96,112},{112,96},{1... | collective-permute-start | bytes 1769480 | tf_op jit(solution)/shard_map/ppermute | solution.py:210
  38.4 2.5 %collective-permute-start.6 = (bf16[2,768,384]{2,1,0:T(8,128)(2,1)}, bf16[2,768,384]{2,1,0:T(8,128)(2,1)S(1)}, u32[]{:S(2)}, u32[]{:S(2)}) collective-permute-start(bf16[2,768,384]{2,1,0:T(8,128)(2,1)} %collective-permute-done.refs_2_.refs_3_), channel_id=1, source_target_pairs={{4,0},{8,4},{12,8},{0,12},{5,1},{9,5},{13,9},{1,13},{6,2},{10,6},{... | collective-permute-start | bytes 3538952 | tf_op jit(solution)/shard_map/ppermute | solution.py:177
  41.0 8.0 %shard_map.38 = (f32[768,768]{1,0:T(8,128)S(1)}, f32[768,384]{1,0:T(8,128)S(1)}) custom-call(s32[8]{0:T(128)S(1)} %convert_element_type.33.refs_0_, bf16[768,384]{1,0:T(8,128)(2,1)S(1)} %get-tuple-element.119.refs_1_, bf16[2,768,384]{2,1,0:T(8,128)(2,1)} %collective-permute-done.refs_2_.refs_3_, ...), custom_call_target="tpu_custom_call" | custom-call | flops 169869312 | bytes 1024 | tf_op jit(solution)/shard_map/pallas_call | solution.py:147
  49.4 12.7 %shard_map.39 = (f32[768,768]{1,0:T(8,128)S(1)}, f32[768,384]{1,0:T(8,128)S(1)}) custom-call(s32[8]{0:T(128)S(1)} %convert_element_type.33.refs_0_, bf16[768,384]{1,0:T(8,128)(2,1)S(1)} %collective-permute-done.4.refs_1_, bf16[2,768,384]{2,1,0:T(8,128)(2,1)S(1)} %constant_dynamic-slice_fusion.3.refs_2_, ...), custom_call_target="tpu_custom_call" | custom-call | flops 283115520 | bytes 1024 | tf_op jit(solution)/shard_map/pallas_call | solution.py:147
  62.1 1.3 collective-permute-done.7.refs_4_
  64.0 2.1 %collective-permute-start.12 = (bf16[2,768,384]{2,1,0:T(8,128)(2,1)S(1)}, bf16[2,768,384]{2,1,0:T(8,128)(2,1)S(1)}, u32[]{:S(2)}, u32[]{:S(2)}) collective-permute-start(bf16[2,768,384]{2,1,0:T(8,128)(2,1)S(1)} %collective-permute-done.7.refs_4_), channel_id=1, source_target_pairs={{4,0},{8,4},{12,8},{0,12},{5,1},{9,5},{13,9},{1,13},{6,2},{10,6},{... | collective-permute-start | bytes 3538952 | tf_op jit(solution)/shard_map/ppermute | solution.py:177
  66.1 6.0 %shard_map.40 = (f32[768,768]{1,0:T(8,128)S(1)}, f32[768,384]{1,0:T(8,128)S(1)}) custom-call(s32[8]{0:T(128)S(1)} %convert_element_type.33.refs_0_, bf16[768,384]{1,0:T(8,128)(2,1)S(1)} %collective-permute-done.4.refs_1_, bf16[2,768,384]{2,1,0:T(8,128)(2,1)S(1)} %collective-permute-done.5.refs_2_, bf16[2,768,384]{2,1,0:T(8,128)(2,1)S(1)} %collective-permute-done.6.refs_3_, ...), custom_call_target="tpu_custom_call" | custom-call | flops 113246208 | bytes 1024 | tf_op jit(solution)/shard_map/pallas_call | solution.py:147
  72.0 7.9 %shard_map.41 = (f32[768,768]{1,0:T(8,128)S(1)}, f32[768,384]{1,0:T(8,128)S(1)}) custom-call(s32[8]{0:T(128)S(1)} %convert_element_type.33.refs_0_, bf16[768,384]{1,0:T(8,128)(2,1)S(1)} %get-tuple-element.119.refs_1_, bf16[2,768,384]{2,1,0:T(8,128)(2,1)S(1)} %collective-permute-done.5.refs_2_, bf16[2,768,384]{2,1,0:T(8,128)(2,1)S(1)} %collective-permute-done.6.refs_3_, ...), custom_call_target="tpu_custom_call" | custom-call | flops 169869312 | bytes 1024 | tf_op jit(solution)/shard_map/pallas_call | solution.py:147
  80.0 5.4 %collective-permute-done.8.refs_2_.refs_3_ = bf16[2,2,768,384]{3,2,1,0:T(8,128)(2,1)S(1)} collective-permute-done((bf16[2,2,768,384]{3,2,1,0:T(8,128)(2,1)S(1)}, bf16[2,2,768,384]{3,2,1,0:T(8,128)(2,1)S(1)}, u32[]{:S(2)}, u32[]{:S(2)}) %collective-permute-start.8) | collective-permute-done | bytes 2359328 | tf_op jit(solution)/shard_map/ppermute | solution.py:208
  85.4 3.8 %shard_map.42 = bf16[384,384]{1,0:T(8,128)(2,1)S(1)} custom-call(s32[8]{0:T(128)S(1)} %convert_element_type.33.refs_0_, bf16[768,384]{1,0:T(8,128)(2,1)S(1)} %collective-permute-done.4.refs_1_, bf16[2,2,768,384]{3,2,1,0:T(8,128)(2,1)S(1)} %collective-permute-done.8.refs_2_.refs_3_, bf16[2,2,768,384]{3,2,1,0:T(8,128)(2,1)S(1)} %collective-permute-done.8.refs_2_.refs_3_, ...), custom_call_target="tpu_custom_call" | custom-call | flops 56623104 | bytes 1024 | tf_op jit(solution)/shard_map/pallas_call | solution.py:147
  89.2 2.1 %collective-permute-start.9 = (bf16[384,384]{1,0:T(8,128)(2,1)S(1)}, bf16[384,384]{1,0:T(8,128)(2,1)S(1)}, u32[]{:S(2)}, u32[]{:S(2)}) collective-permute-start(bf16[384,384]{1,0:T(8,128)(2,1)S(1)} %shard_map.42), channel_id=1, source_target_pairs={{0,16},{16,0},{32,48},{48,32},{64,80},{80,64},{96,112},{112,96},{1... | collective-permute-start | bytes 884744 | tf_op jit(solution)/shard_map/ppermute | solution.py:229
  91.3 3.8 %shard_map.43 = bf16[384,384]{1,0:T(8,128)(2,1)S(1)} custom-call(s32[8]{0:T(128)S(1)} %convert_element_type.33.refs_0_, bf16[768,384]{1,0:T(8,128)(2,1)S(1)} %collective-permute-done.4.refs_1_, bf16[2,2,768,384]{3,2,1,0:T(8,128)(2,1)S(1)} %collective-permute-done.8.refs_2_.refs_3_, bf16[2,2,768,384]{3,2,1,0:T(8,128)(2,1)S(1)} %collective-permute-done.8.refs_2_.refs_3_, ...), custom_call_target="tpu_custom_call" | custom-call | flops 56623104 | bytes 1024 | tf_op jit(solution)/shard_map/pallas_call | solution.py:147
  95.4 5.8 %shard_map.44 = bf16[768,384]{1,0:T(8,128)(2,1)S(1)} custom-call(s32[8]{0:T(128)S(1)} %convert_element_type.33.refs_0_, bf16[768,384]{1,0:T(8,128)(2,1)S(1)} %get-tuple-element.119.refs_1_, bf16[2,768,384]{2,1,0:T(8,128)(2,1)S(1)} %collective-permute-done.11.refs_2_, bf16[2,768,384]{2,1,0:T(8,128)(2,1)S(1)} %collective-permute-done.12.refs_3_, ...), custom_call_target="tpu_custom_call" | custom-call | flops 113246208 | bytes 1024 | tf_op jit(solution)/shard_map/pallas_call | solution.py:147
  101.3 1.6 %collective-permute-done.10 = bf16[384,384]{1,0:T(8,128)(2,1)S(1)} collective-permute-done((bf16[384,384]{1,0:T(8,128)(2,1)S(1)}, bf16[384,384]{1,0:T(8,128)(2,1)S(1)}, u32[]{:S(2)}, u32[]{:S(2)}) %collective-permute-start.10) | collective-permute-done | bytes 294944 | tf_op jit(solution)/shard_map/ppermute | solution.py:229
  103.6 2.7 %collective-permute-start.14 = (bf16[384,768]{1,0:T(8,128)(2,1)S(1)}, bf16[384,768]{1,0:T(8,128)(2,1)S(1)}, u32[]{:S(2)}, u32[]{:S(2)}) collective-permute-start(bf16[384,768]{1,0:T(8,128)(2,1)S(1)} %convolution_convert_fusion.2), channel_id=1, source_target_pairs={{0,1},{1,0},{2,3},{3,2},{4,5},{5,4},{6,7},{7,6},{8,9},{9,8},{10,11... | collective-permute-start | bytes 1769480 | tf_op jit(solution)/shard_map/ppermute | solution.py:244
  106.4 1.1 convolution_convert_fusion
  109.4 2.5 %collective-permute-start.15 = (bf16[384,768]{1,0:T(8,128)(2,1)S(1)}, bf16[384,768]{1,0:T(8,128)(2,1)S(1)}, u32[]{:S(2)}, u32[]{:S(2)}) collective-permute-start(bf16[384,768]{1,0:T(8,128)(2,1)S(1)} %add_convert_fusion.2), channel_id=1, source_target_pairs={{0,2},{1,3},{2,0},{3,1},{4,6},{5,7},{6,4},{7,5},{8,10},{9,11},{10,... | collective-permute-start | bytes 1769480 | tf_op jit(solution)/shard_map/ppermute | solution.py:246
  112.6 1.8 %collective-permute-start.17 = (bf16[384,768]{1,0:T(8,128)(2,1)S(1)}, bf16[384,768]{1,0:T(8,128)(2,1)S(1)}, u32[]{:S(2)}, u32[]{:S(2)}) collective-permute-start(bf16[384,768]{1,0:T(8,128)(2,1)S(1)} %add_convert_fusion.1), channel_id=1, source_target_pairs={{0,2},{1,3},{2,0},{3,1},{4,6},{5,7},{6,4},{7,5},{8,10},{9,11},{10,... | collective-permute-start | bytes 1769480 | tf_op jit(solution)/shard_map/ppermute | solution.py:246
  114.4 1.1 convert_add_fusion
  115.5 10.4 %collective-permute-done.15 = bf16[384,768]{1,0:T(8,128)(2,1)S(1)} collective-permute-done((bf16[384,768]{1,0:T(8,128)(2,1)S(1)}, bf16[384,768]{1,0:T(8,128)(2,1)S(1)}, u32[]{:S(2)}, u32[]{:S(2)}) %collective-permute-start.15) | collective-permute-done | bytes 589856 | tf_op jit(solution)/shard_map/ppermute | solution.py:246
  125.9 12.6 %collective-permute-done.17 = bf16[384,768]{1,0:T(8,128)(2,1)S(1)} collective-permute-done((bf16[384,768]{1,0:T(8,128)(2,1)S(1)}, bf16[384,768]{1,0:T(8,128)(2,1)S(1)}, u32[]{:S(2)}, u32[]{:S(2)}) %collective-permute-start.17) | collective-permute-done | bytes 589856 | tf_op jit(solution)/shard_map/ppermute | solution.py:246
  138.6 1.3 add_convert_fusion
  (34 shorter events, 7.2 us)
Async XLA Ops:
  0.0 1.7 %copy-start = (bf16[2,12,8,8,768]{4,3,2,1,0:T(8,128)(2,1)S(1)}, bf16[2,12,8,8,768]{4,3,2,1,0:T(8,128)(2,1)}, u32[]{:S(2)}) copy-start(bf16[2,12,8,8,768]{4,3,2,1,0:T(8,128)(2,1)} %param.4) | copy-start | bytes 7077892
  2.9 29.2 %collective-permute-start.1 = (bf16[2,768,384]{2,1,0:T(8,128)(2,1)S(1)}, bf16[2,768,384]{2,1,0:T(8,128)(2,1)S(1)}, u32[]{:S(2)}, u32[]{:S(2)}) collective-permute-start(bf16[2,768,384]{2,1,0:T(8,128)(2,1)S(1)} %constant_dynamic-slice_fusion.3.refs_2_), channel_id=1, source_target_pairs={{0,4},{4,8},{8,12},{12,0},{1,5},{5,9},{9,13},{13,1},{2,6},{6,10},{... | collective-permute-start | bytes 3538952 | tf_op jit(solution)/shard_map/ppermute | solution.py:177
  5.1 27.0 %collective-permute-start.2 = (bf16[2,768,384]{2,1,0:T(8,128)(2,1)S(1)}, bf16[2,768,384]{2,1,0:T(8,128)(2,1)S(1)}, u32[]{:S(2)}, u32[]{:S(2)}) collective-permute-start(bf16[2,768,384]{2,1,0:T(8,128)(2,1)S(1)} %constant_dynamic-slice_fusion.3.refs_2_), channel_id=1, source_target_pairs={{4,0},{8,4},{12,8},{0,12},{5,1},{9,5},{13,9},{1,13},{6,2},{10,6},{... | collective-permute-start | bytes 3538952 | tf_op jit(solution)/shard_map/ppermute | solution.py:177
  6.6 30.2 %collective-permute-start.3 = (bf16[2,768,384]{2,1,0:T(8,128)(2,1)S(1)}, bf16[2,768,384]{2,1,0:T(8,128)(2,1)}, u32[]{:S(2)}, u32[]{:S(2)}) collective-permute-start(bf16[2,768,384]{2,1,0:T(8,128)(2,1)S(1)} %constant_dynamic-slice_fusion.3.refs_2_), channel_id=1, source_target_pairs={{0,96},{16,48},{32,0},{48,80},{64,32},{80,112},{96,64},{112,16},{1... | collective-permute-start | bytes 3538952 | tf_op jit(solution)/shard_map/ppermute | solution.py:204
  10.4 26.4 %collective-permute-start = (bf16[2,768,384]{2,1,0:T(8,128)(2,1)}, bf16[2,768,384]{2,1,0:T(8,128)(2,1)}, u32[]{:S(2)}, u32[]{:S(2)}) collective-permute-start(bf16[2,768,384]{2,1,0:T(8,128)(2,1)} %constant_dynamic-slice_fusion.5), channel_id=1, source_target_pairs={{0,16},{16,0},{32,48},{48,32},{64,80},{80,64},{96,112},{112,96},{1... | collective-permute-start | bytes 3538952 | tf_op jit(solution)/shard_map/ppermute | solution.py:202
  13.2 1.3 copy-start.2
  32.4 53.0 %collective-permute-start.8 = (bf16[2,2,768,384]{3,2,1,0:T(8,128)(2,1)S(1)}, bf16[2,2,768,384]{3,2,1,0:T(8,128)(2,1)S(1)}, u32[]{:S(2)}, u32[]{:S(2)}) collective-permute-start(bf16[2,2,768,384]{3,2,1,0:T(8,128)(2,1)S(1)} %pad_maximum_fusion), channel_id=1, source_target_pairs={{0,96},{16,48},{32,0},{48,80},{64,32},{80,112},{96,64},{112,16},{1... | collective-permute-start | bytes 7077896 | tf_op jit(solution)/shard_map/ppermute | solution.py:208
  36.8 26.6 %collective-permute-start.7 = (bf16[2,768,384]{2,1,0:T(8,128)(2,1)}, bf16[2,768,384]{2,1,0:T(8,128)(2,1)S(1)}, u32[]{:S(2)}, u32[]{:S(2)}) collective-permute-start(bf16[2,768,384]{2,1,0:T(8,128)(2,1)} %collective-permute-done.refs_2_.refs_3_), channel_id=1, source_target_pairs={{0,32},{16,112},{32,64},{48,16},{64,96},{80,48},{96,0},{112,80},{1... | collective-permute-start | bytes 3538952 | tf_op jit(solution)/shard_map/ppermute | solution.py:212
  36.8 12.6 %collective-permute-start.4 = (bf16[768,384]{1,0:T(8,128)(2,1)S(1)}, bf16[768,384]{1,0:T(8,128)(2,1)S(1)}, u32[]{:S(2)}, u32[]{:S(2)}) collective-permute-start(bf16[768,384]{1,0:T(8,128)(2,1)S(1)} %get-tuple-element.66), channel_id=1, source_target_pairs={{0,16},{16,0},{32,48},{48,32},{64,80},{80,64},{96,112},{112,96},{1... | collective-permute-start | bytes 1769480 | tf_op jit(solution)/shard_map/ppermute | solution.py:210
  38.3 27.8 %collective-permute-start.5 = (bf16[2,768,384]{2,1,0:T(8,128)(2,1)}, bf16[2,768,384]{2,1,0:T(8,128)(2,1)S(1)}, u32[]{:S(2)}, u32[]{:S(2)}) collective-permute-start(bf16[2,768,384]{2,1,0:T(8,128)(2,1)} %collective-permute-done.refs_2_.refs_3_), channel_id=1, source_target_pairs={{0,4},{4,8},{8,12},{12,0},{1,5},{5,9},{9,13},{13,1},{2,6},{6,10},{... | collective-permute-start | bytes 3538952 | tf_op jit(solution)/shard_map/ppermute | solution.py:177
  38.4 27.6 %collective-permute-start.6 = (bf16[2,768,384]{2,1,0:T(8,128)(2,1)}, bf16[2,768,384]{2,1,0:T(8,128)(2,1)S(1)}, u32[]{:S(2)}, u32[]{:S(2)}) collective-permute-start(bf16[2,768,384]{2,1,0:T(8,128)(2,1)} %collective-permute-done.refs_2_.refs_3_), channel_id=1, source_target_pairs={{4,0},{8,4},{12,8},{0,12},{5,1},{9,5},{13,9},{1,13},{6,2},{10,6},{... | collective-permute-start | bytes 3538952 | tf_op jit(solution)/shard_map/ppermute | solution.py:177
  63.4 32.1 %collective-permute-start.11 = (bf16[2,768,384]{2,1,0:T(8,128)(2,1)S(1)}, bf16[2,768,384]{2,1,0:T(8,128)(2,1)S(1)}, u32[]{:S(2)}, u32[]{:S(2)}) collective-permute-start(bf16[2,768,384]{2,1,0:T(8,128)(2,1)S(1)} %collective-permute-done.7.refs_4_), channel_id=1, source_target_pairs={{0,4},{4,8},{8,12},{12,0},{1,5},{5,9},{9,13},{13,1},{2,6},{6,10},{... | collective-permute-start | bytes 3538952 | tf_op jit(solution)/shard_map/ppermute | solution.py:177
  64.0 31.5 %collective-permute-start.12 = (bf16[2,768,384]{2,1,0:T(8,128)(2,1)S(1)}, bf16[2,768,384]{2,1,0:T(8,128)(2,1)S(1)}, u32[]{:S(2)}, u32[]{:S(2)}) collective-permute-start(bf16[2,768,384]{2,1,0:T(8,128)(2,1)S(1)} %collective-permute-done.7.refs_4_), channel_id=1, source_target_pairs={{4,0},{8,4},{12,8},{0,12},{5,1},{9,5},{13,9},{1,13},{6,2},{10,6},{... | collective-permute-start | bytes 3538952 | tf_op jit(solution)/shard_map/ppermute | solution.py:177
  89.2 12.1 %collective-permute-start.9 = (bf16[384,384]{1,0:T(8,128)(2,1)S(1)}, bf16[384,384]{1,0:T(8,128)(2,1)S(1)}, u32[]{:S(2)}, u32[]{:S(2)}) collective-permute-start(bf16[384,384]{1,0:T(8,128)(2,1)S(1)} %shard_map.42), channel_id=1, source_target_pairs={{0,16},{16,0},{32,48},{48,32},{64,80},{80,64},{96,112},{112,96},{1... | collective-permute-start | bytes 884744 | tf_op jit(solution)/shard_map/ppermute | solution.py:229
  95.1 7.8 %collective-permute-start.10 = (bf16[384,384]{1,0:T(8,128)(2,1)S(1)}, bf16[384,384]{1,0:T(8,128)(2,1)S(1)}, u32[]{:S(2)}, u32[]{:S(2)}) collective-permute-start(bf16[384,384]{1,0:T(8,128)(2,1)S(1)} %shard_map.43), channel_id=1, source_target_pairs={{0,16},{16,0},{32,48},{48,32},{64,80},{80,64},{96,112},{112,96},{1... | collective-permute-start | bytes 884744 | tf_op jit(solution)/shard_map/ppermute | solution.py:229
  103.6 5.1 %collective-permute-start.14 = (bf16[384,768]{1,0:T(8,128)(2,1)S(1)}, bf16[384,768]{1,0:T(8,128)(2,1)S(1)}, u32[]{:S(2)}, u32[]{:S(2)}) collective-permute-start(bf16[384,768]{1,0:T(8,128)(2,1)S(1)} %convolution_convert_fusion.2), channel_id=1, source_target_pairs={{0,1},{1,0},{2,3},{3,2},{4,5},{5,4},{6,7},{7,6},{8,9},{9,8},{10,11... | collective-permute-start | bytes 1769480 | tf_op jit(solution)/shard_map/ppermute | solution.py:244
  107.5 6.9 %collective-permute-start.13 = (bf16[768,768]{1,0:T(8,128)(2,1)S(1)}, bf16[768,768]{1,0:T(8,128)(2,1)S(1)}, u32[]{:S(2)}, u32[]{:S(2)}) collective-permute-start(bf16[768,768]{1,0:T(8,128)(2,1)S(1)} %convolution_convert_fusion), channel_id=1, source_target_pairs={{0,1},{1,0},{2,3},{3,2},{4,5},{5,4},{6,7},{7,6},{8,9},{9,8},{10,11... | collective-permute-start | bytes 3538952 | tf_op jit(solution)/shard_map/ppermute | solution.py:247
  108.2 3.7 %collective-permute-start.16 = (bf16[384,768]{1,0:T(8,128)(2,1)S(1)}, bf16[384,768]{1,0:T(8,128)(2,1)S(1)}, u32[]{:S(2)}, u32[]{:S(2)}) collective-permute-start(bf16[384,768]{1,0:T(8,128)(2,1)S(1)} %convolution_convert_fusion.1), channel_id=1, source_target_pairs={{0,1},{1,0},{2,3},{3,2},{4,5},{5,4},{6,7},{7,6},{8,9},{9,8},{10,11... | collective-permute-start | bytes 1769480 | tf_op jit(solution)/shard_map/ppermute | solution.py:244
  109.4 16.5 %collective-permute-start.15 = (bf16[384,768]{1,0:T(8,128)(2,1)S(1)}, bf16[384,768]{1,0:T(8,128)(2,1)S(1)}, u32[]{:S(2)}, u32[]{:S(2)}) collective-permute-start(bf16[384,768]{1,0:T(8,128)(2,1)S(1)} %add_convert_fusion.2), channel_id=1, source_target_pairs={{0,2},{1,3},{2,0},{3,1},{4,6},{5,7},{6,4},{7,5},{8,10},{9,11},{10,... | collective-permute-start | bytes 1769480 | tf_op jit(solution)/shard_map/ppermute | solution.py:246
  112.6 26.0 %collective-permute-start.17 = (bf16[384,768]{1,0:T(8,128)(2,1)S(1)}, bf16[384,768]{1,0:T(8,128)(2,1)S(1)}, u32[]{:S(2)}, u32[]{:S(2)}) collective-permute-start(bf16[384,768]{1,0:T(8,128)(2,1)S(1)} %add_convert_fusion.1), channel_id=1, source_target_pairs={{0,2},{1,3},{2,0},{3,1},{4,6},{5,7},{6,4},{7,5},{8,10},{9,11},{10,... | collective-permute-start | bytes 1769480 | tf_op jit(solution)/shard_map/ppermute | solution.py:246
  138.5 2.1 %copy-start.1 = (bf16[2,12,8,8,768]{4,3,2,1,0:T(8,128)(2,1)S(1)}, bf16[2,12,8,8,768]{4,3,2,1,0:T(8,128)(2,1)}, u32[]{:S(2)}) copy-start(bf16[2,12,8,8,768]{4,3,2,1,0:T(8,128)(2,1)} %param.4) | copy-start | bytes 7077892
